TPU v7x, 256 devices: a whole 4x4x8 slice. The times are simulated.
256 devices in a mesh: view: 64 (over y, z, x_hi), head: 4 (over x_lo, core).
Axes of the slice: x: 4 (x_hi: 2, x_lo: 2; x = x_hi * 2 + x_lo), y: 4, z: 8, core: 2. Of those that a mesh axis runs over, the one named last changes fastest.
Arguments:
- queries: bfloat16 [256, 1280, 256], P('view', 'head'), may hold values from -6 to 6
- keys: bfloat16 [256, 1280, 256], P('view', 'head'), may hold values from -6 to 6
- values: bfloat16 [256, 1280, 256], P('view', 'head'), may hold values from -6 to 6
- out_grad: bfloat16 [256, 1280, 256], P('view', 'head'), may hold values from -6 to 6
- out_weight: bfloat16 [1280, 1280], P('head'), may hold values from -0.15625 to 0.15625
- visible: int32 [256, 7], P('view'), may hold values from 0 to 1, as said below
Outputs:
- query_grads: bfloat16 [256, 1280, 256], P('view', 'head')
- key_grads: bfloat16 [256, 1280, 256], P('view', 'head')
- value_grads: bfloat16 [256, 1280, 256], P('view', 'head')
Inputs may be any that keep to these rules, and one draw needn't show every extreme that they name: `visible`: 1 wherever the offset's magnitude is 1 or 0; 0 or 1 elsewhere.
All inputs are finite; a program needn't handle non-finite values.
Results may differ from a plain program's by a relative error of at most 0.029.
Values may be sent and summed in bfloat16 or wider, within the bound.
No kernel may reach another device: no remote copies, remote signals or barrier semaphores. Data moves between devices by JAX's collectives and lax.ppermute only.
A program may use at most 128 MiB of HBM per device.

v0:
```python
from functools import partial

import jax
import jax.numpy as jnp
from jax import lax
from jax.sharding import PartitionSpec as P

DH = 64
R = 3


def padded(array, sides, width):
    for axis, dim in sides:
        devices, length = (lax.axis_size(axis), array.shape[dim])
        up = [(i, (i + 1) % devices) for i in range(devices)]
        down = [(j, i) for i, j in up]
        last = lax.slice_in_dim(array, length - width, length, axis=dim)
        initial = lax.slice_in_dim(array, 0, width, axis=dim)
        before = lax.ppermute(last, axis, up)
        after = lax.ppermute(initial, axis, down)
        array = jnp.concatenate([before, array, after], axis=dim)
    return array


def from_behind(block, axis, distance):
    devices = range(lax.axis_size(axis))
    route = [((i - distance) % len(devices), i) for i in devices]
    return lax.ppermute(block, axis, route)


def local(queries, keys, values, out_grad, out_weight, visible):
    half = jnp.bfloat16
    single = jnp.float32
    count, width, tokens = queries.shape
    heads = width // DH
    span = 2 * R + 1
    scale = DH ** (-0.5)
    attn_grad = jnp.einsum(
        "ij,vjt->vit",
        out_weight,
        lax.all_gather(out_grad, "head", axis=1, tiled=True),
        preferred_element_type=single,
    ).astype(half)
    pair = jnp.stack((keys, values))
    rims = padded(pair, (("view", 1),), R)

    def query_side(index, with_parts):
        key_win = lax.dynamic_slice_in_dim(rims[0], index, span, 0).reshape(span, heads, DH, tokens)
        value_win = lax.dynamic_slice_in_dim(rims[1], index, span, 0).reshape(
            span, heads, DH, tokens
        )
        query_now = lax.dynamic_index_in_dim(queries, index, 0, False).reshape(heads, DH, tokens)
        grad_now = lax.dynamic_index_in_dim(attn_grad, index, 0, False).reshape(heads, DH, tokens)
        seen = lax.dynamic_index_in_dim(visible, index, 0, False) > 0
        scores = (
            jnp.einsum("hdt,ohdu->htou", query_now, key_win, preferred_element_type=single) * scale
        )
        scores = jnp.where(seen[None, None, :, None], scores, -jnp.inf)
        top = jnp.max(scores, axis=(2, 3), keepdims=True)
        lse = top + jnp.log(jnp.sum(jnp.exp(scores - top), axis=(2, 3), keepdims=True))
        probs = jnp.exp(scores - lse)
        probs_low = probs.astype(half)
        output = jnp.einsum(
            "htou,ohdu->hdt", probs_low, value_win, preferred_element_type=single
        ).astype(half)
        delta = jnp.sum(grad_now.astype(single) * output.astype(single), axis=1)
        dprob = jnp.einsum("hdt,ohdu->htou", grad_now, value_win, preferred_element_type=single)
        dscore = (probs * (dprob - delta[:, :, None, None])).astype(half)
        query_grad = (
            scale * jnp.einsum("htou,ohdu->hdt", dscore, key_win, preferred_element_type=single)
        ).astype(half)
        query_grad = query_grad.reshape(width, tokens)
        key_part = jnp.einsum("htou,hdt->ohdu", dscore, query_now, preferred_element_type=single)
        value_part = jnp.einsum(
            "htou,hdt->ohdu", probs_low, grad_now, preferred_element_type=single
        )
        both = jnp.stack(
            (key_part.reshape(span, width, tokens), value_part.reshape(span, width, tokens))
        )
        return (query_grad, both)

    indices = jnp.arange(count, dtype=jnp.int32)
    query_grads, parts = lax.map(partial(query_side, with_parts=True), indices)
    total = sum(
        (
            jnp.pad(parts[:, :, offset], ((offset, span - 1 - offset), (0, 0), (0, 0), (0, 0)))
            for offset in range(span)
        )
    )
    left_rim = total[:R]
    right_rim = total[count + R :]
    from_right = from_behind(left_rim, "view", -1)
    from_left = from_behind(right_rim, "view", 1)
    owned = total[R : R + count]
    owned = owned.at[:R].add(from_left).at[count - R :].add(from_right)
    key_grads = (scale * owned[:, 0]).astype(half)
    value_grads = owned[:, 1].astype(half)
    return (query_grads, key_grads, value_grads)


def solution(mesh):
    return jax.shard_map(
        local,
        mesh=mesh,
        in_specs=(
            P("view", "head", None),
            P("view", "head", None),
            P("view", "head", None),
            P("view", "head", None),
            P("head", None),
            P("view", None),
        ),
        out_specs=(P("view", "head", None), P("view", "head", None), P("view", "head", None)),
        check_vma=False,
    )
```

profile of v0, /device:TPU:1, one launch (start us, length us, event | category | flops | bytes accessed | tf_op | source)
XLA Modules:
  0.0 300.6 jit_solution(9190674113419562902)
XLA Ops:
  7.9 2.9 fusion.37
  10.9 3.6 %collective-permute-start = (bf16[2,3,320,256]{3,2,1,0:T(8,128)(2,1)}, bf16[2,3,320,256]{3,2,1,0:T(8,128)(2,1)S(1)}, u32[]{:S(2)}, u32[]{:S(2)}) collective-permute-start(bf16[2,3,320,256]{3,2,1,0:T(8,128)(2,1)} %get-tuple-element.105), channel_id=1, source_target_pairs={{0,4},{4,8},{8,12},{12,16},{16,20},{20,24},{24,28},{28,32},{32,36}... | collective-permute-start | bytes 2949128 | tf_op jit(solution)/shard_map/ppermute | solution.py:19
  14.4 7.7 %collective-permute-start.1 = (bf16[2,3,320,256]{3,2,1,0:T(8,128)(2,1)}, bf16[2,3,320,256]{3,2,1,0:T(8,128)(2,1)}, u32[]{:S(2)}, u32[]{:S(2)}) collective-permute-start(bf16[2,3,320,256]{3,2,1,0:T(8,128)(2,1)} %get-tuple-element.106), channel_id=1, source_target_pairs={{4,0},{8,4},{12,8},{16,12},{20,16},{24,20},{28,24},{32,28},{36,32}... | collective-permute-start | bytes 2949128 | tf_op jit(solution)/shard_map/ppermute | solution.py:20
  22.2 51.3 %collective-permute-done = bf16[2,3,320,256]{3,2,1,0:T(8,128)(2,1)S(1)} collective-permute-done((bf16[2,3,320,256]{3,2,1,0:T(8,128)(2,1)}, bf16[2,3,320,256]{3,2,1,0:T(8,128)(2,1)S(1)}, u32[]{:S(2)}, u32[]{:S(2)}) %collective-permute-start) | collective-permute-done | bytes 983072 | tf_op jit(solution)/shard_map/ppermute | solution.py:19
  73.4 3.2 %collective-permute-done.1 = bf16[2,3,320,256]{3,2,1,0:T(8,128)(2,1)} collective-permute-done((bf16[2,3,320,256]{3,2,1,0:T(8,128)(2,1)}, bf16[2,3,320,256]{3,2,1,0:T(8,128)(2,1)}, u32[]{:S(2)}, u32[]{:S(2)}) %collective-permute-start.1) | collective-permute-done | bytes 983072 | tf_op jit(solution)/shard_map/ppermute | solution.py:20
  76.7 2.9 pad_maximum_fusion
  79.7 2.8 fusion.36
  82.6 100.0 %while.14 = (s32[]{:T(128)}, bf16[4,320,256]{2,1,0:T(8,128)(2,1)S(1)}, f32[4,2,7,320,256]{4,3,0,1,2:T(8,128)}, bf16[2,10,320,256]{3,2,1,0:T(8,128)(2,1)}, s32[4]...) while((s32[]{:T(128)}, ...), condition=%wide.region_4.5_spmd, body=%wide.region_0.4_spmd.sunk | while | flops 1802319360 | bytes 104909080 | solution.py:83
  86.6 0.7 compare_bitcast_fusion.2
  87.3 0.9 constant_dynamic-slice_fusion.8
  88.2 2.1 fusion.79
  90.5 1.9 fusion.80
  92.5 1.9 exponential_reduce_fusion.2
  94.4 1.9 fusion.81
  96.2 0.9 fusion.82
  97.1 3.4 %multiply_convert_fusion.2 = bf16[5,256,7,256]{1,3,2,0:T(8,128)(2,1)S(1)} fusion(f32[5,256,7,256]{1,3,2,0:T(8,128)S(1)} %get-tuple-element.168, f32[5,256]{1,0:T(8,128)S(1)} %fusion.82, f32[5,256]{1,0:T(8,128)S(1)} %log_add_fusion.2, pred[7]{0:T(512)(128)(4,1)S(1)} %compare_bitcast_fusion.2, bf16[5,64,256,1]{2,1,3,0:T(8,128)(2,1)S(1)} %bitcast.132, ...), kind=kOutput, calls=%fused_computation.clone.1 | convolution fusion | flops 307363840 | bytes 15083527 | tf_op jit(solution)/shard_map/while/body/eval_jaxpr/hdt,ohdu->htou/dot_general | solution.py:67
  100.6 1.5 convolution_bitcast_fusion.4
  102.1 0.9 fusion.83
  103.0 1.5 convolution_bitcast_fusion.5
  105.0 2.7 copy_dynamic-update-slice_fusion.2
  111.6 0.7 compare_bitcast_fusion.2
  112.3 0.9 constant_dynamic-slice_fusion.8
  113.2 2.1 fusion.79
  115.5 1.9 fusion.80
  117.5 1.9 exponential_reduce_fusion.2
  119.4 1.9 fusion.81
  121.2 0.9 fusion.82
  122.2 3.4 %multiply_convert_fusion.2 = bf16[5,256,7,256]{1,3,2,0:T(8,128)(2,1)S(1)} fusion(f32[5,256,7,256]{1,3,2,0:T(8,128)S(1)} %get-tuple-element.168, f32[5,256]{1,0:T(8,128)S(1)} %fusion.82, f32[5,256]{1,0:T(8,128)S(1)} %log_add_fusion.2, pred[7]{0:T(512)(128)(4,1)S(1)} %compare_bitcast_fusion.2, bf16[5,64,256,1]{2,1,3,0:T(8,128)(2,1)S(1)} %bitcast.132, ...), kind=kOutput, calls=%fused_computation.clone.1 | convolution fusion | flops 307363840 | bytes 15083527 | tf_op jit(solution)/shard_map/while/body/eval_jaxpr/hdt,ohdu->htou/dot_general | solution.py:67
  125.6 1.5 convolution_bitcast_fusion.4
  127.1 0.9 fusion.83
  128.0 1.5 convolution_bitcast_fusion.5
  130.0 2.6 copy_dynamic-update-slice_fusion.2
  136.5 0.7 compare_bitcast_fusion.2
  137.2 0.9 constant_dynamic-slice_fusion.8
  138.1 2.1 fusion.79
  140.4 1.9 fusion.80
  142.4 1.9 exponential_reduce_fusion.2
  144.3 1.9 fusion.81
  146.1 0.9 fusion.82
  147.0 3.4 %multiply_convert_fusion.2 = bf16[5,256,7,256]{1,3,2,0:T(8,128)(2,1)S(1)} fusion(f32[5,256,7,256]{1,3,2,0:T(8,128)S(1)} %get-tuple-element.168, f32[5,256]{1,0:T(8,128)S(1)} %fusion.82, f32[5,256]{1,0:T(8,128)S(1)} %log_add_fusion.2, pred[7]{0:T(512)(128)(4,1)S(1)} %compare_bitcast_fusion.2, bf16[5,64,256,1]{2,1,3,0:T(8,128)(2,1)S(1)} %bitcast.132, ...), kind=kOutput, calls=%fused_computation.clone.1 | convolution fusion | flops 307363840 | bytes 15083527 | tf_op jit(solution)/shard_map/while/body/eval_jaxpr/hdt,ohdu->htou/dot_general | solution.py:67
  150.5 1.5 convolution_bitcast_fusion.4
  152.0 0.9 fusion.83
  152.9 1.5 convolution_bitcast_fusion.5
  154.9 2.6 copy_dynamic-update-slice_fusion.2
  161.4 0.7 compare_bitcast_fusion.2
  162.1 0.9 constant_dynamic-slice_fusion.8
  163.0 2.1 fusion.79
  165.3 1.9 fusion.80
  167.3 1.9 exponential_reduce_fusion.2
  169.2 1.9 fusion.81
  171.1 0.9 fusion.82
  172.0 3.4 %multiply_convert_fusion.2 = bf16[5,256,7,256]{1,3,2,0:T(8,128)(2,1)S(1)} fusion(f32[5,256,7,256]{1,3,2,0:T(8,128)S(1)} %get-tuple-element.168, f32[5,256]{1,0:T(8,128)S(1)} %fusion.82, f32[5,256]{1,0:T(8,128)S(1)} %log_add_fusion.2, pred[7]{0:T(512)(128)(4,1)S(1)} %compare_bitcast_fusion.2, bf16[5,64,256,1]{2,1,3,0:T(8,128)(2,1)S(1)} %bitcast.132, ...), kind=kOutput, calls=%fused_computation.clone.1 | convolution fusion | flops 307363840 | bytes 15083527 | tf_op jit(solution)/shard_map/while/body/eval_jaxpr/hdt,ohdu->htou/dot_general | solution.py:67
  175.4 1.5 convolution_bitcast_fusion.4
  176.9 0.9 fusion.83
  177.8 1.5 convolution_bitcast_fusion.5
  179.9 2.7 copy_dynamic-update-slice_fusion.2
  182.5 11.0 %slice_bitcast_fusion.6 = (f32[4,2,320,256]{3,2,0,1:T(8,128)S(1)}, f32[4,2,320,256]{3,2,0,1:T(8,128)S(1)}, f32[4,2,320,256]{3,2,0,1:T(8,128)S(1)}, f32[4,2,320,2...) fusion(f32[4,2,7,320,256]{4,3,0,1,2:T(8,128)} %get-tuple-element.71), kind=kLoop, calls=%fused_computation.41 | loop fusion | bytes 36700160 | tf_op jit(solution)/shard_map/squeeze | solution.py:86
  193.5 4.9 %pad_add_fusion = f32[10,2,320,256]{3,2,0,1:T(8,128)S(1)} fusion(f32[4,2,320,256]{3,2,0,1:T(8,128)} %get-tuple-element.102, f32[4,2,320,256]{3,2,0,1:T(8,128)S(1)} %get-tuple-element.97, f32[4,2,320,256]{3,2,0,1:T(8,128)S(1)} %get-tuple-element.98, f32[4,2,320,256]{3,2,0,1:T(8,128)} %get-tuple-element.99, f32[4,2,320,256]{3,2,0,1:T(8,128)} %get-tuple-element.100, ...), kind=kLoop, calls=%fused_computation.33 | loop fusion | flops 9830400 | bytes 24903680 | tf_op jit(solution)/shard_map/add | solution.py:84
  198.7 3.6 %collective-permute-start.2 = (f32[3,2,320,256]{3,2,0,1:T(8,128)S(1)}, f32[3,2,320,256]{3,2,0,1:T(8,128)S(1)}, u32[]{:S(2)}, u32[]{:S(2)}) collective-permute-start(f32[3,2,320,256]{3,2,0,1:T(8,128)S(1)} %get-tuple-element.104), channel_id=1, source_target_pairs={{252,0},{0,4},{4,8},{8,12},{12,16},{16,20},{20,24},{24,28},{28,32}... | collective-permute-start | bytes 5898248 | tf_op jit(solution)/shard_map/ppermute | solution.py:28
  202.2 6.9 %collective-permute-start.3 = (f32[3,2,320,256]{3,2,0,1:T(8,128)S(1)}, f32[3,2,320,256]{3,2,0,1:T(8,128)S(1)}, u32[]{:S(2)}, u32[]{:S(2)}) collective-permute-start(f32[3,2,320,256]{3,2,0,1:T(8,128)S(1)} %get-tuple-element.103), channel_id=1, source_target_pairs={{4,0},{8,4},{12,8},{16,12},{20,16},{24,20},{28,24},{32,28},{36,32}... | collective-permute-start | bytes 5898248 | tf_op jit(solution)/shard_map/ppermute | solution.py:28
  209.4 76.2 %collective-permute-done.2 = f32[3,2,320,256]{3,2,0,1:T(8,128)S(1)} collective-permute-done((f32[3,2,320,256]{3,2,0,1:T(8,128)S(1)}, f32[3,2,320,256]{3,2,0,1:T(8,128)S(1)}, u32[]{:S(2)}, u32[]{:S(2)}) %collective-permute-start.2) | collective-permute-done | bytes 1966112 | tf_op jit(solution)/shard_map/ppermute | solution.py:28
  285.9 5.5 %collective-permute-done.3 = f32[3,2,320,256]{3,2,0,1:T(8,128)S(1)} collective-permute-done((f32[3,2,320,256]{3,2,0,1:T(8,128)S(1)}, f32[3,2,320,256]{3,2,0,1:T(8,128)S(1)}, u32[]{:S(2)}, u32[]{:S(2)}) %collective-permute-start.3) | collective-permute-done | bytes 1966112 | tf_op jit(solution)/shard_map/ppermute | solution.py:28
  291.9 0.9 fusion.40
  292.8 1.0 fusion.39
  (46 shorter events, 7.1 us)
Async XLA Ops:
  7.2 72.6 %copy-start = (bf16[320,1280]{1,0:T(8,128)(2,1)S(1)}, bf16[320,1280]{1,0:T(8,128)(2,1)}, u32[]{:S(2)}) copy-start(bf16[320,1280]{1,0:T(8,128)(2,1)} %param.16) | copy-start | bytes 2457604
  7.2 69.5 %copy-start.3 = (bf16[4,320,256]{2,1,0:T(8,128)(2,1)S(1)}, bf16[4,320,256]{2,1,0:T(8,128)(2,1)}, u32[]{:S(2)}) copy-start(bf16[4,320,256]{2,1,0:T(8,128)(2,1)} %param.14) | copy-start | bytes 1966084
  7.2 69.5 %copy-start.2 = (bf16[4,320,256]{2,1,0:T(8,128)(2,1)S(1)}, bf16[4,320,256]{2,1,0:T(8,128)(2,1)}, u32[]{:S(2)}) copy-start(bf16[4,320,256]{2,1,0:T(8,128)(2,1)} %param.13) | copy-start | bytes 1966084
  7.2 72.5 %all-gather.2.cloned.1.call-start = ((), (), s32[]{:S(2)}) async-start(), calls=%async_computation | async-start | bytes 3276800 | tf_op jit(solution)/shard_map/all_gather | solution.py:41
  10.9 62.6 %collective-permute-start = (bf16[2,3,320,256]{3,2,1,0:T(8,128)(2,1)}, bf16[2,3,320,256]{3,2,1,0:T(8,128)(2,1)S(1)}, u32[]{:S(2)}, u32[]{:S(2)}) collective-permute-start(bf16[2,3,320,256]{3,2,1,0:T(8,128)(2,1)} %get-tuple-element.105), channel_id=1, source_target_pairs={{0,4},{4,8},{8,12},{12,16},{16,20},{20,24},{24,28},{28,32},{32,36}... | collective-permute-start | bytes 2949128 | tf_op jit(solution)/shard_map/ppermute | solution.py:19
  14.4 62.2 %collective-permute-start.1 = (bf16[2,3,320,256]{3,2,1,0:T(8,128)(2,1)}, bf16[2,3,320,256]{3,2,1,0:T(8,128)(2,1)}, u32[]{:S(2)}, u32[]{:S(2)}) collective-permute-start(bf16[2,3,320,256]{3,2,1,0:T(8,128)(2,1)} %get-tuple-element.106), channel_id=1, source_target_pairs={{4,0},{8,4},{12,8},{16,12},{20,16},{24,20},{28,24},{32,28},{36,32}... | collective-permute-start | bytes 2949128 | tf_op jit(solution)/shard_map/ppermute | solution.py:20
  79.6 3.0 copy-start.4
  182.5 11.0 %copy-start.5 = (bf16[4,320,256]{2,1,0:T(8,128)(2,1)}, bf16[4,320,256]{2,1,0:T(8,128)(2,1)S(1)}, u32[]{:S(2)}) copy-start(bf16[4,320,256]{2,1,0:T(8,128)(2,1)S(1)} %get-tuple-element.67) | copy-start | bytes 1966084
  198.7 86.9 %collective-permute-start.2 = (f32[3,2,320,256]{3,2,0,1:T(8,128)S(1)}, f32[3,2,320,256]{3,2,0,1:T(8,128)S(1)}, u32[]{:S(2)}, u32[]{:S(2)}) collective-permute-start(f32[3,2,320,256]{3,2,0,1:T(8,128)S(1)} %get-tuple-element.104), channel_id=1, source_target_pairs={{252,0},{0,4},{4,8},{8,12},{12,16},{16,20},{20,24},{24,28},{28,32}... | collective-permute-start | bytes 5898248 | tf_op jit(solution)/shard_map/ppermute | solution.py:28
  202.2 89.1 %collective-permute-start.3 = (f32[3,2,320,256]{3,2,0,1:T(8,128)S(1)}, f32[3,2,320,256]{3,2,0,1:T(8,128)S(1)}, u32[]{:S(2)}, u32[]{:S(2)}) collective-permute-start(f32[3,2,320,256]{3,2,0,1:T(8,128)S(1)} %get-tuple-element.103), channel_id=1, source_target_pairs={{4,0},{8,4},{12,8},{16,12},{20,16},{24,20},{28,24},{32,28},{36,32}... | collective-permute-start | bytes 5898248 | tf_op jit(solution)/shard_map/ppermute | solution.py:28
  285.6 8.1 %copy-start.1 = (bf16[320,1280]{1,0:T(8,128)(2,1)S(1)}, bf16[320,1280]{1,0:T(8,128)(2,1)}, u32[]{:S(2)}) copy-start(bf16[320,1280]{1,0:T(8,128)(2,1)} %param.16) | copy-start | bytes 2457604
Sparse Core Ops, SparseCore 0:
  9.8 69.8 all-gather.1
where the time goes:
time: 301 us
  waiting for transfers between devices  137 us (46%)
  matrix products  43.6 us (14%)
  other arithmetic  40.8 us (14%)
  local copies, waits for them, and re-layouts  29.7 us (10%)
  starting transfers between devices  21.9 us (7%)
  between operations  14.1 us (5%)
  loops' own time  13.5 us (4%)
    ppermute x2, waiting for transfers between devices, from_behind(): return lax.ppermute(block, axis, route)  81.7 us
    ppermute x1, waiting for transfers between devices, padded(): before = lax.ppermute(last, axis, up)  51.3 us
    dot_general x4, matrix products, query_side(): jnp.einsum('hdt,ohdu->htou', grad_now, value_win, preferred_element_type=...  13.6 us
    another operation x1, loops' own time, local(): query_grads, parts = lax.map(partial(query_side, with_parts=True), indices)  13.5 us
    squeeze x1, local copies, waits for them, and re-layouts, local(): parts[:, :, offset]  11 us
    dynamic_update_slice x4, other arithmetic, local(): query_grads, parts = lax.map(partial(query_side, with_parts=True), indices)  10.6 us
    ppermute x2, starting transfers between devices, from_behind(): return lax.ppermute(block, axis, route)  10.5 us
    slice x4, local copies, waits for them, and re-layouts, query_side(): rims[1]  8.55 us
  transfers between devices with their start and end apart: 5, of which 5 were waited for; matrix products, arithmetic and copies ran while one was open for 2% of the time, Pallas kernels for 0%

commit v1 on v0

v1 whole, which is shorter than its diff:
```python
from functools import partial

import jax
import jax.numpy as jnp
from jax import lax
from jax.experimental import pallas as pl
from jax.experimental.pallas import tpu as pltpu
from jax.sharding import PartitionSpec as P

DH = 64
R = 3
CHUNKS = (2, 3)


def attn_kernel(vis_ref, q_ref, g_ref, k_ref, v_ref, hp_ref, hn_ref,
                dq_ref, own_ref, prev_ref, next_ref,
                kvt, kcat, acc, s_ref, dp_ref, e_ref, ds_ref):
    f32=jnp.float32; bf=jnp.bfloat16
    T=q_ref.shape[2]; count=q_ref.shape[0]; span=2*R+1; W=count+2*R
    for w in range(W):
        if w<R: kw,vw=hp_ref[0,w],hp_ref[1,w]
        elif w<R+count: kw,vw=k_ref[w-R],v_ref[w-R]
        else: kw,vw=hn_ref[0,w-R-count],hn_ref[1,w-R-count]
        kvt[w*T:(w+1)*T,:]=jnp.concatenate([kw,vw],axis=0).T
        kcat[:,w*T:(w+1)*T]=kw
    lane=lax.broadcasted_iota(jnp.int32,(T,2*DH),1)
    zero=jnp.zeros((DH,T),bf)
    for i in range(count):
        q=q_ref[i]*jnp.asarray(0.125,bf); g=g_ref[i]
        q0=jnp.concatenate([q,zero],axis=0); g0=jnp.concatenate([zero,g],axis=0)
        top=None; seen=[]
        for o in range(span):
            w=i+o
            s=jnp.dot(kvt[w*T:(w+1)*T,:],q0,preferred_element_type=f32)
            s_ref[o*T:(o+1)*T,:]=s
            bm=jnp.max(s.reshape(T//8,8,T),axis=0)
            on=vis_ref[i,o]>0
            seen.append(on)
            if abs(o-R)>1: bm=jnp.where(on,bm,-jnp.inf)
            top=bm if top is None else jnp.maximum(top,bm)
        m=jnp.max(top,axis=0,keepdims=True)
        l8=jnp.zeros((8,T),f32); r8=jnp.zeros((8,T),f32)
        for o in range(span):
            w=i+o
            dp=jnp.dot(kvt[w*T:(w+1)*T,:],g0,preferred_element_type=f32)
            mo=jnp.where(seen[o],m,jnp.inf) if abs(o-R)>1 else m
            e=jnp.exp(s_ref[o*T:(o+1)*T,:]-mo)
            dp_ref[o*T:(o+1)*T,:]=dp
            s_ref[o*T:(o+1)*T,:]=e
            e_ref[o*T:(o+1)*T,:]=e.astype(bf)
            l8=l8+jnp.sum(e.reshape(T//8,8,T),axis=0)
            r8=r8+jnp.sum((e*dp).reshape(T//8,8,T),axis=0)
        inv=1.0/jnp.sum(l8,axis=0,keepdims=True)
        delta=jnp.sum(r8,axis=0,keepdims=True)*inv
        qg=(jnp.concatenate([q,g],axis=0).astype(f32)*inv).astype(bf).T
        qt=jnp.where(lane<DH,qg,0); gt=jnp.where(lane<DH,0,qg)
        for o in range(span):
            w=i+o
            sl=slice(o*T,(o+1)*T)
            ds=(s_ref[sl,:]*(dp_ref[sl,:]-delta)).astype(bf)
            ds_ref[sl,:]=ds
            part=jnp.dot(ds,qt,preferred_element_type=f32)+jnp.dot(e_ref[sl,:],gt,preferred_element_type=f32)
            aw=slice(w*T,(w+1)*T)
            if o==span-1 or i==0: acc[aw,:]=part
            else: acc[aw,:]+=part
        dq=jnp.dot(kcat[:,i*T:(i+span)*T],ds_ref[...],preferred_element_type=f32)
        dq_ref[i]=(dq*(inv*0.125)).astype(bf)
    for w in range(W):
        t=acc[w*T:(w+1)*T,:].T
        if w<R: prev_ref[0,w]=t[:DH].astype(bf); prev_ref[1,w]=t[DH:].astype(bf)
        elif w<R+count: own_ref[0,w-R]=t[:DH]; own_ref[1,w-R]=t[DH:]
        else: next_ref[0,w-R-count]=t[:DH].astype(bf); next_ref[1,w-R-count]=t[DH:].astype(bf)

def attn(vis,q,g,k,v,hp,hn,first,heads,kernel=attn_kernel):
    count,_,T=q.shape; span=2*R+1; W=count+2*R
    own=pl.BlockSpec((count,DH,T),lambda h:(0,first+h,0))
    halo=pl.BlockSpec((2,R,DH,T),lambda h:(0,0,h,0))
    n=heads*DH
    f32=jnp.float32; bf=jnp.bfloat16
    return pl.pallas_call(kernel,grid=(heads,),
      in_specs=[pl.BlockSpec(memory_space=pltpu.SMEM),own,own,own,own,halo,halo],
      out_specs=[pl.BlockSpec((count,DH,T),lambda h:(0,h,0)),pl.BlockSpec((2,count,DH,T),lambda h:(0,0,h,0)),halo,halo],
      out_shape=[jax.ShapeDtypeStruct((count,n,T),bf),jax.ShapeDtypeStruct((2,count,n,T),f32),
                 jax.ShapeDtypeStruct((2,R,n,T),bf),jax.ShapeDtypeStruct((2,R,n,T),bf)],
      scratch_shapes=[pltpu.VMEM((W*T,2*DH),bf),pltpu.VMEM((DH,W*T),bf),pltpu.VMEM((W*T,2*DH),f32),
        pltpu.VMEM((span*T,T),f32),pltpu.VMEM((span*T,T),f32),pltpu.VMEM((span*T,T),bf),pltpu.VMEM((span*T,T),bf)],
      compiler_params=pltpu.CompilerParams(vmem_limit_bytes=48*2**20),
      cost_estimate=pl.CostEstimate(flops=heads*count*span*5*2*T*T*DH*4,bytes_accessed=heads*1000000,transcendentals=0),
    )(vis,q,g,k,v,hp,hn)


def route(move):
    views, heads = lax.axis_size("view"), lax.axis_size("head")
    pairs = []
    for g in range(views):
        for h in range(heads):
            to_g, to_h = move(g, h)
            pairs.append((g * heads + h, to_g % views * heads + to_h))
    return pairs


def send(array, move):
    return lax.ppermute(array, ("view", "head"), route(move))


def after(array, *others):
    return lax.optimization_barrier((array, *others))[0]


def local(queries, keys, values, out_grad, out_weight, visible):
    half = jnp.bfloat16
    single = jnp.float32
    count, width, tokens = queries.shape
    me = lax.axis_index("head")
    beside = send(out_grad, lambda g, h: (g, h ^ 2))

    def halos(first, heads, *wait):
        rows = slice(first * DH, (first + heads) * DH)
        last = jnp.stack((keys[count - R :, rows], values[count - R :, rows]))
        initial = jnp.stack((keys[:R, rows], values[:R, rows]))
        if wait:
            last, initial = lax.optimization_barrier((last, initial, *wait))[:2]
        return send(last, lambda g, h: (g + 1, h)), send(initial, lambda g, h: (g - 1, h))

    spans = []
    for heads in CHUNKS:
        spans.append((sum(n for _, n in spans), heads))
    rims = [halos(*spans[0])]
    other = send(jnp.stack((out_grad, beside)), lambda g, h: (g, h ^ 1))
    rims += [halos(*part, beside) for part in spans[1:]]
    order = [me, me ^ 2, me ^ 1, me ^ 3]
    weight = jnp.concatenate(
        [lax.dynamic_slice_in_dim(out_weight, source * width, width, 1) for source in order], 1
    )
    gathered = jnp.concatenate((out_grad, beside, other[0], other[1]), 1)
    attn_grad = jnp.einsum(
        "ij,vjt->vit", weight, gathered, preferred_element_type=single
    ).astype(half)
    query_grads, owned = [], []
    for (first, heads), (before, behind) in zip(spans, rims):
        dq, own, prev, nxt = attn(
            visible, queries, attn_grad, keys, values, before, behind, first, heads
        )
        query_grads.append(dq)
        from_right = send(prev, lambda g, h: (g - 1, h))
        from_left = send(nxt, lambda g, h: (g + 1, h))
        owned.append((own, from_left, from_right))
    totals = []
    for own, from_left, from_right in owned:
        own = own.at[:, :R].add(from_left.astype(single))
        own = own.at[:, count - R :].add(from_right.astype(single))
        totals.append(own)
    total = jnp.concatenate(totals, 2).astype(half)
    return jnp.concatenate(query_grads, 1), total[0], total[1]


def solution(mesh):
    return jax.shard_map(
        local,
        mesh=mesh,
        in_specs=(
            P("view", "head", None),
            P("view", "head", None),
            P("view", "head", None),
            P("view", "head", None),
            P("head", None),
            P("view", None),
        ),
        out_specs=(P("view", "head", None), P("view", "head", None), P("view", "head", None)),
        check_vma=False,
    )
```

time: 301 us -> 135 us (0.45)
  waiting for transfers between devices: 137 us -> 44.1 us
  matrix products: 43.6 us -> 1.24 us
  Pallas kernels: 0 us -> 38.7 us
  other arithmetic: 40.8 us -> 7.28 us
  local copies, waits for them, and re-layouts: 29.7 us -> 5.13 us
  starting transfers between devices: 21.9 us -> 37.5 us
  loops' own time: 13.5 us -> 0 us
  between operations: 14.1 us -> 0.83 us
    ppermute x4 -> x10, waiting for transfers between devices: 136 us -> 44.1 us  [send(): return lax.ppermute(array, ('view', 'head'), route(move))]
    dot_general x25 -> x1, matrix products: 43.6 us -> 1.24 us  [local(): jnp.einsum('ij,vjt->vit', weight, gathered, preferred_element_type=single)]
    pallas_call x0 -> x2, Pallas kernels: none -> 38.7 us  [attn(): pl.pallas_call(kernel, grid=(heads,), in_specs=[pl.BlockSpec(memory_space...]
    ppermute x4 -> x10, starting transfers between devices: 21.8 us -> 37.5 us  [send(): return lax.ppermute(array, ('view', 'head'), route(move))]
    another operation x1 -> x0, loops' own time: 13.5 us -> none  [local(): query_grads, parts = lax.map(partial(query_side, with_parts=True), indices)]
    squeeze x1, local copies, waits for them, and re-layouts: 11 us -> 0.09 us  [local(): gathered = jnp.concatenate((out_grad, beside, other[0], other[1]), 1)]
    dynamic_update_slice x4 -> x0, other arithmetic: 10.6 us -> none  [local(): query_grads, parts = lax.map(partial(query_side, with_parts=True), indices)]
    slice x6 -> x0, local copies, waits for them, and re-layouts: 8.99 us -> none  [the longest x4 8.55 us: query_side(): rims[1]]
  transfers between devices with their start and end apart: 5 -> 10, of which waited for: 5 -> 5; matrix products, arithmetic and copies ran while one was open for 2% -> 7% of each run, Pallas kernels for 0% -> 29%
where the time goes in v1:
time: 135 us
  waiting for transfers between devices  44.1 us (33%)
  Pallas kernels  38.7 us (29%)
  starting transfers between devices  37.5 us (28%)
  other arithmetic  7.28 us (5%)
  local copies, waits for them, and re-layouts  5.13 us (4%)
    ppermute x10, waiting for transfers between devices, send(): return lax.ppermute(array, ('view', 'head'), route(move))  44.1 us
    pallas_call x2, Pallas kernels, attn(): pl.pallas_call(kernel, grid=(heads,), in_specs=[pl.BlockSpec(memory_space...  38.7 us
    ppermute x10, starting transfers between devices, send(): return lax.ppermute(array, ('view', 'head'), route(move))  37.5 us
  transfers between devices with their start and end apart: 10, of which 5 were waited for; matrix products, arithmetic and copies ran while one was open for 7% of the time, Pallas kernels for 29%

profile of v1, /device:TPU:1, one launch (start us, length us, event | category | flops | bytes accessed | tf_op | source)
XLA Modules:
  0.0 134.7 jit_solution(8247352333537187175)
XLA Ops:
  0.6 2.1 %collective-permute-start = (bf16[4,320,256]{2,1,0:T(8,128)(2,1)}, bf16[4,320,256]{2,1,0:T(8,128)(2,1)S(1)}, u32[]{:S(2)}, u32[]{:S(2)}) collective-permute-start(bf16[4,320,256]{2,1,0:T(8,128)(2,1)} %param.17), channel_id=1, source_target_pairs={{0,2},{1,3},{2,0},{3,1},{4,6},{5,7},{6,4},{7,5},{8,10},{9,11},{10,... | collective-permute-start | bytes 1966088 | tf_op jit(solution)/shard_map/ppermute | solution.py:103
  2.8 13.4 %collective-permute-done = bf16[4,320,256]{2,1,0:T(8,128)(2,1)S(1)} collective-permute-done((bf16[4,320,256]{2,1,0:T(8,128)(2,1)}, bf16[4,320,256]{2,1,0:T(8,128)(2,1)S(1)}, u32[]{:S(2)}, u32[]{:S(2)}) %collective-permute-start) | collective-permute-done | bytes 655392 | tf_op jit(solution)/shard_map/ppermute | solution.py:103
  16.2 0.0 copy-start.7
  16.2 0.0 copy-start
  16.2 0.0 copy-start.1
  16.2 2.5 %pad_maximum_fusion = bf16[2,4,320,256]{3,2,1,0:T(8,128)(2,1)} fusion(bf16[1,4,320,256]{3,2,1,0:T(8,128)(2,1)S(1)} %bitcast.32, bf16[1,4,320,256]{3,2,1,0:T(8,128)(2,1)} %bitcast.31), kind=kLoop, calls=%fused_computation.9 | loop fusion | flops 655360 | bytes 2621440 | tf_op jit(solution)/shard_map/stack | solution.py:129
  18.7 0.0 copy-done.7
  18.7 2.5 %collective-permute-start.1 = (bf16[2,4,320,256]{3,2,1,0:T(8,128)(2,1)}, bf16[2,4,320,256]{3,2,1,0:T(8,128)(2,1)S(1)}, u32[]{:S(2)}, u32[]{:S(2)}) collective-permute-start(bf16[2,4,320,256]{3,2,1,0:T(8,128)(2,1)} %pad_maximum_fusion), channel_id=1, source_target_pairs={{0,1},{1,0},{2,3},{3,2},{4,5},{5,4},{6,7},{7,6},{8,9},{9,8},{10,11... | collective-permute-start | bytes 3932168 | tf_op jit(solution)/shard_map/ppermute | solution.py:103
  21.2 0.0 copy-done
  21.2 0.0 copy-done.1
  21.2 0.1 slice_bitcast_fusion.6
  21.3 0.8 pad_maximum_fusion.5
  22.1 3.0 %collective-permute-start.2 = (bf16[2,3,128,256]{3,2,1,0:T(8,128)(2,1)}, bf16[2,3,128,256]{3,2,1,0:T(8,128)(2,1)S(1)}, u32[]{:S(2)}, u32[]{:S(2)}) collective-permute-start(bf16[2,3,128,256]{3,2,1,0:T(8,128)(2,1)} %pad_maximum_fusion.5), channel_id=1, source_target_pairs={{0,4},{1,5},{2,6},{3,7},{4,8},{5,9},{6,10},{7,11},{8,12},{9,13},{1... | collective-permute-start | bytes 1179656 | tf_op jit(solution)/shard_map/ppermute | solution.py:103
  25.1 0.8 pad_maximum_fusion.6
  25.8 7.7 %collective-permute-start.3 = (bf16[2,3,128,256]{3,2,1,0:T(8,128)(2,1)}, bf16[2,3,128,256]{3,2,1,0:T(8,128)(2,1)S(1)}, u32[]{:S(2)}, u32[]{:S(2)}) collective-permute-start(bf16[2,3,128,256]{3,2,1,0:T(8,128)(2,1)} %pad_maximum_fusion.6), channel_id=1, source_target_pairs={{0,252},{1,253},{2,254},{3,255},{4,0},{5,1},{6,2},{7,3},{8,4},{9,5... | collective-permute-start | bytes 1179656 | tf_op jit(solution)/shard_map/ppermute | solution.py:103
  33.6 2.6 %constant_dynamic-slice_fusion = (bf16[320,320]{1,0:T(8,128)(2,1)}, bf16[320,320]{1,0:T(8,128)(2,1)}, bf16[320,320]{1,0:T(8,128)(2,1)}, bf16[320,320]{1,0:T(8,128)(2,1)}) fusion(bf16[320,1280]{1,0:T(8,128)(2,1)} %param.18, s32[]{:T(128)S(6)} %select_n.15, s32[]{:T(128)S(6)} %select_n.13, s32[]{:T(128)S(6)} %select_n.12, s32[]{:T(128)S(6)} %select_n.14), kind=kLoop, calls=%fused_computation.39 | loop fusion | bytes 1638416 | tf_op jit(solution)/shard_map/dynamic_slice | solution.py:133
  36.2 2.2 %concatenate.22 = bf16[320,1280]{1,0:T(8,128)(2,1)} concatenate(bf16[320,320]{1,0:T(8,128)(2,1)} %get-tuple-element.77, bf16[320,320]{1,0:T(8,128)(2,1)} %get-tuple-element.76, bf16[320,320]{1,0:T(8,128)(2,1)} %get-tuple-element.78, bf16[320,320]{1,0:T(8,128)(2,1)} %get-tuple-element.75), dimensions={1} | concatenate | bytes 1638400 | tf_op jit(solution)/shard_map/concatenate | solution.py:132
  38.5 0.1 pad_maximum_fusion.3
  38.7 0.0 copy-start.5
  38.7 0.0 copy-start.6
  38.7 0.0 copy-start.8
  38.7 0.1 collective-permute-start.4
  38.8 7.2 %collective-permute-start.5 = (bf16[2,3,192,256]{3,2,1,0:T(8,128)(2,1)S(1)}, bf16[2,3,192,256]{3,2,1,0:T(8,128)(2,1)S(1)}, u32[]{:S(2)}, u32[]{:S(2)}) collective-permute-start(bf16[2,3,192,256]{3,2,1,0:T(8,128)(2,1)S(1)} %get-tuple-element.63), channel_id=1, source_target_pairs={{0,252},{1,253},{2,254},{3,255},{4,0},{5,1},{6,2},{7,3},{8,4},{9,5... | collective-permute-start | bytes 1769480 | tf_op jit(solution)/shard_map/ppermute | solution.py:103
  46.0 0.0 collective-permute-done.1
  46.0 0.1 slice_bitcast_fusion.1
  46.0 0.0 copy-done.5
  46.1 0.0 copy-done.6
  46.1 0.0 copy-done.8
  46.1 0.0 copy-start.2
  46.1 0.0 copy-start.3
  46.1 1.2 fusion.11.g_ref
  47.3 7.6 %collective-permute-done.2.hp_ref = bf16[2,3,128,256]{3,2,1,0:T(8,128)(2,1)S(1)} collective-permute-done((bf16[2,3,128,256]{3,2,1,0:T(8,128)(2,1)}, bf16[2,3,128,256]{3,2,1,0:T(8,128)(2,1)S(1)}, u32[]{:S(2)}, u32[]{:S(2)}) %collective-permute-start.2) | collective-permute-done | bytes 393248 | tf_op jit(solution)/shard_map/ppermute | solution.py:103
  55.0 4.1 %collective-permute-done.3.hn_ref = bf16[2,3,128,256]{3,2,1,0:T(8,128)(2,1)S(1)} collective-permute-done((bf16[2,3,128,256]{3,2,1,0:T(8,128)(2,1)}, bf16[2,3,128,256]{3,2,1,0:T(8,128)(2,1)S(1)}, u32[]{:S(2)}, u32[]{:S(2)}) %collective-permute-start.3) | collective-permute-done | bytes 393248 | tf_op jit(solution)/shard_map/ppermute | solution.py:103
  59.0 0.0 copy-done.2
  59.0 0.0 copy-done.3
  59.0 15.3 %shard_map.85 = (bf16[4,128,256]{2,1,0:T(8,128)(2,1)S(1)}, f32[2,4,128,256]{3,2,1,0:T(8,128)S(1)}, bf16[2,3,128,256]{3,2,1,0:T(8,128)(2,1)S(1)}, bf16[2,3,128,256]{3,2,1,0:T(8,128)(2,1)S(1)}) custom-call(s32[4,7]{1,0:T(4,128)S(1)} %copy-done.3, bf16[4,320,256]{2,1,0:T(8,128)(2,1)S(1)} %copy-done.2, bf16[4,320,256]{2,1,0:T(8,128)(2,1)S(1)} %fusion.11.g_ref, ...), custom_call_target="tpu_custom_call" | custom-call | flops 9395240960 | bytes 2000000 | tf_op jit(solution)/shard_map/pallas_call | solution.py:80
  74.3 0.1 collective-permute-start.6
  74.4 7.6 %collective-permute-start.7 = (bf16[2,3,128,256]{3,2,1,0:T(8,128)(2,1)S(1)}, bf16[2,3,128,256]{3,2,1,0:T(8,128)(2,1)S(1)}, u32[]{:S(2)}, u32[]{:S(2)}) collective-permute-start(bf16[2,3,128,256]{3,2,1,0:T(8,128)(2,1)S(1)} %get-tuple-element.67), channel_id=1, source_target_pairs={{0,252},{1,253},{2,254},{3,255},{4,0},{5,1},{6,2},{7,3},{8,4},{9,5... | collective-permute-start | bytes 1179656 | tf_op jit(solution)/shard_map/ppermute | solution.py:103
  82.0 0.0 collective-permute-done.4.hp_ref
  82.0 0.0 collective-permute-done.5.hn_ref
  82.0 23.4 %shard_map.86 = (bf16[4,192,256]{2,1,0:T(8,128)(2,1)S(1)}, f32[2,4,192,256]{3,2,1,0:T(8,128)}, bf16[2,3,192,256]{3,2,1,0:T(8,128)(2,1)S(1)}, bf16[2,3,192,256]{3,2,1,0:T(8,128)(2,1)S(1)}) custom-call(s32[4,7]{1,0:T(4,128)S(1)} %copy-done.3, bf16[4,320,256]{2,1,0:T(8,128)(2,1)S(1)} %copy-done.2, bf16[4,320,256]{2,1,0:T(8,128)(2,1)S(1)} %fusion.11.g_ref, ...), custom_call_target="tpu_custom_call" | custom-call | flops 14092861440 | bytes 3000000 | tf_op jit(solution)/shard_map/pallas_call | solution.py:80
  105.4 0.0 collective-permute-start.8
  105.4 7.2 %collective-permute-start.9 = (bf16[2,3,192,256]{3,2,1,0:T(8,128)(2,1)S(1)}, bf16[2,3,192,256]{3,2,1,0:T(8,128)(2,1)S(1)}, u32[]{:S(2)}, u32[]{:S(2)}) collective-permute-start(bf16[2,3,192,256]{3,2,1,0:T(8,128)(2,1)S(1)} %get-tuple-element.70), channel_id=1, source_target_pairs={{0,252},{1,253},{2,254},{3,255},{4,0},{5,1},{6,2},{7,3},{8,4},{9,5... | collective-permute-start | bytes 1769480 | tf_op jit(solution)/shard_map/ppermute | solution.py:103
  112.6 0.9 pad_maximum_fusion.2
  113.5 0.0 collective-permute-done.6
  113.5 0.2 add_dynamic-update-slice_fusion.1
  113.7 0.0 copy-start.4
  113.7 0.0 collective-permute-done.7
  113.7 0.2 fusion.16
  113.9 0.1 convert.6
  113.9 16.7 %collective-permute-done.8 = bf16[2,3,192,256]{3,2,1,0:T(8,128)(2,1)S(1)} collective-permute-done((bf16[2,3,192,256]{3,2,1,0:T(8,128)(2,1)S(1)}, bf16[2,3,192,256]{3,2,1,0:T(8,128)(2,1)S(1)}, u32[]{:S(2)}, u32[]{:S(2)}) %collective-permute-start.8) | collective-permute-done | bytes 589856 | tf_op jit(solution)/shard_map/ppermute | solution.py:103
  130.6 0.0 copy-done.4
  130.6 0.3 add_dynamic-update-slice_fusion
  130.9 2.3 %collective-permute-done.9 = bf16[2,3,192,256]{3,2,1,0:T(8,128)(2,1)S(1)} collective-permute-done((bf16[2,3,192,256]{3,2,1,0:T(8,128)(2,1)S(1)}, bf16[2,3,192,256]{3,2,1,0:T(8,128)(2,1)S(1)}, u32[]{:S(2)}, u32[]{:S(2)}) %collective-permute-start.9) | collective-permute-done | bytes 589856 | tf_op jit(solution)/shard_map/ppermute | solution.py:103
  133.2 0.3 fusion.14
  133.5 0.1 convert.7
  133.6 1.1 fusion.19
  (2 shorter events, 0.1 us)
Async XLA Ops:
  0.6 15.6 %collective-permute-start = (bf16[4,320,256]{2,1,0:T(8,128)(2,1)}, bf16[4,320,256]{2,1,0:T(8,128)(2,1)S(1)}, u32[]{:S(2)}, u32[]{:S(2)}) collective-permute-start(bf16[4,320,256]{2,1,0:T(8,128)(2,1)} %param.17), channel_id=1, source_target_pairs={{0,2},{1,3},{2,0},{3,1},{4,6},{5,7},{6,4},{7,5},{8,10},{9,11},{10,... | collective-permute-start | bytes 1966088 | tf_op jit(solution)/shard_map/ppermute | solution.py:103
  16.2 2.6 %copy-start.7 = (bf16[4,320,256]{2,1,0:T(8,128)(2,1)}, bf16[4,320,256]{2,1,0:T(8,128)(2,1)S(1)}, u32[]{:S(2)}) copy-start(bf16[4,320,256]{2,1,0:T(8,128)(2,1)S(1)} %collective-permute-done) | copy-start | bytes 1966084
  16.2 5.0 %copy-start = (bf16[4,320,256]{2,1,0:T(8,128)(2,1)S(1)}, bf16[4,320,256]{2,1,0:T(8,128)(2,1)}, u32[]{:S(2)}) copy-start(bf16[4,320,256]{2,1,0:T(8,128)(2,1)} %k_ref.3) | copy-start | bytes 1966084
  16.2 5.0 %copy-start.1 = (bf16[4,320,256]{2,1,0:T(8,128)(2,1)S(1)}, bf16[4,320,256]{2,1,0:T(8,128)(2,1)}, u32[]{:S(2)}) copy-start(bf16[4,320,256]{2,1,0:T(8,128)(2,1)} %v_ref.3) | copy-start | bytes 1966084
  18.7 27.2 %collective-permute-start.1 = (bf16[2,4,320,256]{3,2,1,0:T(8,128)(2,1)}, bf16[2,4,320,256]{3,2,1,0:T(8,128)(2,1)S(1)}, u32[]{:S(2)}, u32[]{:S(2)}) collective-permute-start(bf16[2,4,320,256]{3,2,1,0:T(8,128)(2,1)} %pad_maximum_fusion), channel_id=1, source_target_pairs={{0,1},{1,0},{2,3},{3,2},{4,5},{5,4},{6,7},{7,6},{8,9},{9,8},{10,11... | collective-permute-start | bytes 3932168 | tf_op jit(solution)/shard_map/ppermute | solution.py:103
  22.1 32.9 %collective-permute-start.2 = (bf16[2,3,128,256]{3,2,1,0:T(8,128)(2,1)}, bf16[2,3,128,256]{3,2,1,0:T(8,128)(2,1)S(1)}, u32[]{:S(2)}, u32[]{:S(2)}) collective-permute-start(bf16[2,3,128,256]{3,2,1,0:T(8,128)(2,1)} %pad_maximum_fusion.5), channel_id=1, source_target_pairs={{0,4},{1,5},{2,6},{3,7},{4,8},{5,9},{6,10},{7,11},{8,12},{9,13},{1... | collective-permute-start | bytes 1179656 | tf_op jit(solution)/shard_map/ppermute | solution.py:103
  25.8 33.2 %collective-permute-start.3 = (bf16[2,3,128,256]{3,2,1,0:T(8,128)(2,1)}, bf16[2,3,128,256]{3,2,1,0:T(8,128)(2,1)S(1)}, u32[]{:S(2)}, u32[]{:S(2)}) collective-permute-start(bf16[2,3,128,256]{3,2,1,0:T(8,128)(2,1)} %pad_maximum_fusion.6), channel_id=1, source_target_pairs={{0,252},{1,253},{2,254},{3,255},{4,0},{5,1},{6,2},{7,3},{8,4},{9,5... | collective-permute-start | bytes 1179656 | tf_op jit(solution)/shard_map/ppermute | solution.py:103
  38.7 7.4 %copy-start.5 = (bf16[320,1280]{1,0:T(8,128)(2,1)S(1)}, bf16[320,1280]{1,0:T(8,128)(2,1)}, u32[]{:S(2)}) copy-start(bf16[320,1280]{1,0:T(8,128)(2,1)} %concatenate.22) | copy-start | bytes 2457604
  38.7 7.4 %copy-start.6 = (bf16[4,320,256]{2,1,0:T(8,128)(2,1)S(1)}, bf16[4,320,256]{2,1,0:T(8,128)(2,1)}, u32[]{:S(2)}) copy-start(bf16[4,320,256]{2,1,0:T(8,128)(2,1)} %param.17) | copy-start | bytes 1966084
  38.7 7.4 %copy-start.8 = (bf16[4,320,256]{2,1,0:T(8,128)(2,1)S(1)}, bf16[4,320,256]{2,1,0:T(8,128)(2,1)}, u32[]{:S(2)}) copy-start(bf16[4,320,256]{2,1,0:T(8,128)(2,1)} %copy-done.7) | copy-start | bytes 1966084
  38.7 43.3 %collective-permute-start.4 = (bf16[2,3,192,256]{3,2,1,0:T(8,128)(2,1)S(1)}, bf16[2,3,192,256]{3,2,1,0:T(8,128)(2,1)S(1)}, u32[]{:S(2)}, u32[]{:S(2)}) collective-permute-start(bf16[2,3,192,256]{3,2,1,0:T(8,128)(2,1)S(1)} %get-tuple-element.62), channel_id=1, source_target_pairs={{0,4},{1,5},{2,6},{3,7},{4,8},{5,9},{6,10},{7,11},{8,12},{9,13},{1... | collective-permute-start | bytes 1769480 | tf_op jit(solution)/shard_map/ppermute | solution.py:103
  38.8 43.2 %collective-permute-start.5 = (bf16[2,3,192,256]{3,2,1,0:T(8,128)(2,1)S(1)}, bf16[2,3,192,256]{3,2,1,0:T(8,128)(2,1)S(1)}, u32[]{:S(2)}, u32[]{:S(2)}) collective-permute-start(bf16[2,3,192,256]{3,2,1,0:T(8,128)(2,1)S(1)} %get-tuple-element.63), channel_id=1, source_target_pairs={{0,252},{1,253},{2,254},{3,255},{4,0},{5,1},{6,2},{7,3},{8,4},{9,5... | collective-permute-start | bytes 1769480 | tf_op jit(solution)/shard_map/ppermute | solution.py:103
  46.1 13.0 %copy-start.2 = (bf16[4,320,256]{2,1,0:T(8,128)(2,1)S(1)}, bf16[4,320,256]{2,1,0:T(8,128)(2,1)}, u32[]{:S(2)}) copy-start(bf16[4,320,256]{2,1,0:T(8,128)(2,1)} %q_ref.3) | copy-start | bytes 1966084
  46.1 13.0 %copy-start.3 = (s32[4,7]{1,0:T(4,128)S(1)}, s32[4,7]{1,0:T(4,128)}, u32[]{:S(2)}) copy-start(s32[4,7]{1,0:T(4,128)} %vis_ref.3) | copy-start | bytes 340
  74.3 39.1 %collective-permute-start.6 = (bf16[2,3,128,256]{3,2,1,0:T(8,128)(2,1)S(1)}, bf16[2,3,128,256]{3,2,1,0:T(8,128)(2,1)S(1)}, u32[]{:S(2)}, u32[]{:S(2)}) collective-permute-start(bf16[2,3,128,256]{3,2,1,0:T(8,128)(2,1)S(1)} %get-tuple-element.66), channel_id=1, source_target_pairs={{0,4},{1,5},{2,6},{3,7},{4,8},{5,9},{6,10},{7,11},{8,12},{9,13},{1... | collective-permute-start | bytes 1179656 | tf_op jit(solution)/shard_map/ppermute | solution.py:103
  74.4 39.3 %collective-permute-start.7 = (bf16[2,3,128,256]{3,2,1,0:T(8,128)(2,1)S(1)}, bf16[2,3,128,256]{3,2,1,0:T(8,128)(2,1)S(1)}, u32[]{:S(2)}, u32[]{:S(2)}) collective-permute-start(bf16[2,3,128,256]{3,2,1,0:T(8,128)(2,1)S(1)} %get-tuple-element.67), channel_id=1, source_target_pairs={{0,252},{1,253},{2,254},{3,255},{4,0},{5,1},{6,2},{7,3},{8,4},{9,5... | collective-permute-start | bytes 1179656 | tf_op jit(solution)/shard_map/ppermute | solution.py:103
  105.4 25.2 %collective-permute-start.8 = (bf16[2,3,192,256]{3,2,1,0:T(8,128)(2,1)S(1)}, bf16[2,3,192,256]{3,2,1,0:T(8,128)(2,1)S(1)}, u32[]{:S(2)}, u32[]{:S(2)}) collective-permute-start(bf16[2,3,192,256]{3,2,1,0:T(8,128)(2,1)S(1)} %get-tuple-element.69), channel_id=1, source_target_pairs={{0,4},{1,5},{2,6},{3,7},{4,8},{5,9},{6,10},{7,11},{8,12},{9,13},{1... | collective-permute-start | bytes 1769480 | tf_op jit(solution)/shard_map/ppermute | solution.py:103
  105.4 27.8 %collective-permute-start.9 = (bf16[2,3,192,256]{3,2,1,0:T(8,128)(2,1)S(1)}, bf16[2,3,192,256]{3,2,1,0:T(8,128)(2,1)S(1)}, u32[]{:S(2)}, u32[]{:S(2)}) collective-permute-start(bf16[2,3,192,256]{3,2,1,0:T(8,128)(2,1)S(1)} %get-tuple-element.70), channel_id=1, source_target_pairs={{0,252},{1,253},{2,254},{3,255},{4,0},{5,1},{6,2},{7,3},{8,4},{9,5... | collective-permute-start | bytes 1769480 | tf_op jit(solution)/shard_map/ppermute | solution.py:103
  113.7 16.9 %copy-start.4 = (f32[2,4,192,256]{3,2,1,0:T(8,128)S(1)}, f32[2,4,192,256]{3,2,1,0:T(8,128)}, u32[]{:S(2)}) copy-start(f32[2,4,192,256]{3,2,1,0:T(8,128)} %get-tuple-element.68) | copy-start | bytes 4718596

commit v2 on v0

v2 whole, which is shorter than its diff:
```python
import jax
import jax.numpy as jnp
from jax import lax
from jax.experimental import pallas as pl
from jax.experimental.pallas import tpu as pltpu
from jax.sharding import PartitionSpec as P

DH = 64
R = 3
STRIP = 64
GROUPS = ((2, False), (3, False))
PARTS = ((2, False), (2, False), (1, False))


def attn_kernel(
    vis_ref, col_ref, q_ref, g_ref, k_ref, v_ref, near_ref, far_ref, *rest
):
    (
        dq_ref, own_ref, near_out, far_out,
        kvt, kcat, acc, s_ref, dp_ref, pe_ref,
    ) = rest[-10:]
    single = jnp.float32
    half = jnp.bfloat16
    count, _, T = q_ref.shape
    span = 2 * R + 1
    first = col_ref[0] == 0
    skip = col_ref[0] if near_ref.shape[1] > R else 0

    def window(w):
        if w < R:
            return [jnp.where(first, far_ref[n, w], near_ref[n, skip + w]) for n in (0, 1)]
        if w < R + count:
            return k_ref[w - R], v_ref[w - R]
        w -= R + count
        return [jnp.where(first, near_ref[n, skip + w], far_ref[n, w]) for n in (0, 1)]

    for w in range(count + 2 * R):
        key, value = window(w)
        rows = slice(w * T, (w + 1) * T)
        kvt[rows, :] = jnp.concatenate([key, value], axis=0).T
        kcat[:, rows] = key
    lane = lax.broadcasted_iota(jnp.int32, (T, 2 * DH), 1)
    zero = jnp.zeros((DH, T), half)
    state = {}

    def fold(x, op):
        return op(x.reshape(x.shape[0] // 8, 8, T), axis=0)

    def begin(i):
        q = q_ref[i] * jnp.asarray(DH**-0.5, half)
        g = g_ref[i]
        state[i] = dict(
            q=q, g=g, q0=jnp.concatenate([q, zero], axis=0),
            g0=jnp.concatenate([zero, g], axis=0), top=None,
            total=jnp.zeros((8, T), single), cross=jnp.zeros((8, T), single))

    def score(i, o):
        z, w, b = state[i], i + o, i % 2
        s = jnp.dot(kvt[w * T : (w + 1) * T, :], z["q0"], preferred_element_type=single)
        s_ref[b, o * T : (o + 1) * T, :] = s
        best = fold(s, jnp.max)
        if abs(o - R) > 1:
            best = jnp.where(vis_ref[i, o] > 0, best, -jnp.inf)
        z["top"] = best if z["top"] is None else jnp.maximum(z["top"], best)

    def weigh(i, o):
        z, w, b = state[i], i + o, i % 2
        if o == 0:
            z["top"] = jnp.max(z["top"], axis=0, keepdims=True)
        top = z["top"]
        floor = jnp.where(vis_ref[i, o] > 0, top, jnp.inf) if abs(o - R) > 1 else top
        dp = jnp.dot(kvt[w * T : (w + 1) * T, :], z["g0"], preferred_element_type=single)
        for c in range(0, T, STRIP):
            rows = slice(o * T + c, o * T + c + STRIP)
            e = jnp.exp(s_ref[b, rows, :] - floor)
            z["total"] += fold(e, jnp.sum)
            pe_ref[b, rows, T:] = e.astype(half)
            d = dp[c : c + STRIP]
            z["cross"] += fold(e * d, jnp.sum)
            dp_ref[b, rows, :] = d.astype(dp_ref.dtype)

    def norm(i):
        z = state[i]
        z["inv"] = inv = 1.0 / jnp.sum(z["total"], axis=0, keepdims=True)
        z["delta"] = jnp.sum(z["cross"], axis=0, keepdims=True) * inv
        qg = (jnp.concatenate([z["q"], z["g"]], axis=0).astype(single) * inv).astype(half).T
        z["qgt"] = jnp.concatenate([jnp.where(lane < DH, qg, 0), jnp.where(lane < DH, 0, qg)], axis=0)
        z["dq"] = None

    def spread(i, o):
        z, w, b = state[i], i + o, i % 2
        for c in range(0, T, STRIP):
            rows = slice(o * T + c, o * T + c + STRIP)
            ds = pe_ref[b, rows, T:].astype(single) * (dp_ref[b, rows, :].astype(single) - z["delta"])
            pe_ref[b, rows, :T] = ds.astype(half)
        rows = slice(o * T, (o + 1) * T)
        part = jnp.dot(pe_ref[b, rows, :], z["qgt"], preferred_element_type=single)
        there = slice(w * T, (w + 1) * T)
        if o == span - 1 or i == 0:
            acc[there, :] = part
        else:
            acc[there, :] += part
        dq = jnp.dot(kcat[:, there], pe_ref[b, rows, :T], preferred_element_type=single)
        z["dq"] = dq if z["dq"] is None else z["dq"] + dq

    def finish(i):
        z = state[i]
        dq_ref[i] = (z["dq"] * (z["inv"] * DH**-0.5)).astype(half)

    for step in range(count + 2):
        for at, start in ((step, begin), (step - 2, norm)):
            if 0 <= at < count:
                start(at)
        for o in range(span):
            for at, stage in ((step - 2, spread), (step - 1, weigh), (step, score)):
                if 0 <= at < count:
                    stage(at, o)
        if step >= 2:
            finish(step - 2)

    def taken(w):
        return acc[w * T : (w + 1) * T, :].T

    for w in range(count):
        both = taken(R + w)
        own_ref[0, w], own_ref[1, w] = both[:DH], both[DH:]
    for w in range(R):
        low, high = taken(w), taken(R + count + w)
        for ref, both in (
            (near_out, jnp.where(first, high, low).astype(half)),
            (far_out, jnp.where(first, low, high).astype(half)),
        ):
            ref[0, w], ref[1, w] = both[:DH], both[DH:]


def attn(visible, column, queries, grads, keys, values, near, far, first, skipped, heads, so_far):
    count, _, T = queries.shape
    span = 2 * R + 1
    windows = (count + 2 * R) * T
    single = jnp.float32
    half = jnp.bfloat16

    def block(*lead, at=0):
        zeros = (0,) * len(lead)
        return pl.BlockSpec((*lead, DH, T), lambda h: (*zeros, at + h, 0))

    own = block(count, at=first)
    smem = pl.BlockSpec(memory_space=pltpu.SMEM)
    width = heads * DH
    return pl.pallas_call(
        attn_kernel,
        grid=(heads,),
        in_specs=[smem, smem, own, own, own, own, block(2, near.shape[1], at=skipped), block(2, R, at=skipped)]
        + [pl.BlockSpec(memory_space=pl.ANY)] * len(so_far),
        out_specs=[own, block(2, count, at=first), block(2, R), block(2, R)],
        out_shape=[
            jax.ShapeDtypeStruct(queries.shape, half),
            jax.ShapeDtypeStruct((2, *queries.shape), single),
            jax.ShapeDtypeStruct((2, R, width, T), half),
            jax.ShapeDtypeStruct((2, R, width, T), half),
        ],
        scratch_shapes=[
            pltpu.VMEM((windows, 2 * DH), half),
            pltpu.VMEM((DH, windows), half),
            pltpu.VMEM((windows, 2 * DH), single),
            pltpu.VMEM((2, span * T, T), single),
            pltpu.VMEM((2, span * T, T), half),
            pltpu.VMEM((2, span * T, 2 * T), half),
        ],
        input_output_aliases={8 + n: n for n in range(len(so_far))},
        compiler_params=pltpu.CompilerParams(vmem_limit_bytes=40 * 2**20),
        cost_estimate=pl.CostEstimate(
            flops=heads * count * span * 40 * T * T * DH,
            bytes_accessed=heads * 4 * 2**20,
            transcendentals=heads * count * span * T * T,
        ),
    )(visible, column, queries, grads, keys, values, near, far, *so_far)

def send(array, move, label):
    views, heads = lax.axis_size("view"), lax.axis_size("head")
    pairs = []
    for g in range(views):
        for h in range(heads):
            to_g, to_h = move(g, h)
            pairs.append((g * heads + h, to_g % views * heads + to_h))
    with jax.named_scope(label):
        return lax.ppermute(array, ("view", "head"), pairs)


def to_near(g, h):
    return g ^ 1, h


def to_far(g, h):
    return (g - 1, h) if g % 2 == 0 else (g + 1, h)


def along(g, h):
    return (g + 2, h) if g % 2 == 0 else (g - 2, h)


def against(g, h):
    return (g - 2, h) if g % 2 == 0 else (g + 2, h)


def local(queries, keys, values, out_grad, out_weight, visible):
    half = jnp.bfloat16
    single = jnp.float32
    count, width, tokens = queries.shape
    me = lax.axis_index("head")
    column = lax.axis_index("view") % 2

    def views(array, at):
        return lax.dynamic_slice_in_dim(array, at, R, 1)

    def spans(parts):
        start = 0
        for heads, shared in parts:
            yield start, heads, shared
            start += heads

    def halos(first, heads, shared, wait):
        rows = slice(first * DH, (first + heads) * DH)
        pair = jnp.stack((keys[:, rows], values[:, rows]))
        if wait is not None:
            pair = lax.optimization_barrier((pair, wait))[0]
        if shared:
            near = send(pair, to_near, f"in_near_{first}")
            far = send(views(near, 1 - column), along, f"in_far_{first}")
        else:
            near = send(views(pair, 1 - column), to_near, f"in_near_{first}")
            far = send(views(pair, column), to_far, f"in_far_{first}")
        return near, far

    beside = send(out_grad, lambda g, h: (g, h ^ 2), "beside")
    groups = list(spans(GROUPS))
    rims = [halos(*groups[0], None)]
    twin = send(out_grad, lambda g, h: (g, h ^ 1), "twin")
    across = send(beside, lambda g, h: (g, h ^ 1), "across")
    for part in groups[1:]:
        rims.append(halos(*part, beside))
    order = [me, me ^ 1, me ^ 2, me ^ 3]
    weight = jnp.concatenate(
        [lax.dynamic_slice_in_dim(out_weight, source * width, width, 1) for source in order], 1
    )
    gathered = jnp.concatenate((out_grad, twin, beside, across), 1)
    attn_grad = jnp.einsum(
        "ij,vjt->vit", weight, gathered, preferred_element_type=single
    ).astype(half)
    so_far, backs = (), []
    for first, heads, shared in spans(PARTS):
        group = max(n for n, (start, _, _) in enumerate(groups) if start <= first)
        near, far = rims[group]
        if len(backs) > 1:
            near, *backs[-2] = lax.optimization_barrier((near, *backs[-2]))
        query_grads, own, near_part, far_part = attn(
            visible, column[None], queries, attn_grad, keys, values, near, far, first,
            first - groups[group][0], heads, so_far,
        )
        so_far = (query_grads, own)
        if first == 0:
            near_part, far_part, *rims[1] = lax.optimization_barrier(
                (near_part, far_part, *rims[1])
            )
        if shared:
            back = send(far_part, against, f"out_far_{first}")
            both = jnp.zeros((2, count, *near_part.shape[2:]), single)
            place = lambda part, at: lax.dynamic_update_slice_in_dim(
                both, part.astype(single), at, 1
            )
            both = (place(near_part, column) + place(back, 1 - column)).astype(half)
            backs.append([send(both, to_near, f"out_near_{first}")])
        else:
            backs.append([send(near_part, to_near, f"out_near_{first}"), send(far_part, to_far, f"out_far_{first}")])
    tail = lax.optimization_barrier((*backs[-2], *backs[-1]))
    backs[-2:] = [tail[: len(backs[-2])], tail[len(backs[-2]) :]]
    sums = []
    for (first, heads, _), (near, *far) in zip(spans(PARTS), backs):
        mine = own[:, :, first * DH : (first + heads) * DH]
        if not far:
            mine = mine + near.astype(single)
        else:
            low = jnp.where(column == 0, far[0], near).astype(single)
            high = jnp.where(column == 0, near, far[0]).astype(single)
            mine = mine.at[:, :R].add(low).at[:, count - R :].add(high)
        sums.append(mine.astype(half))
    total = jnp.concatenate(sums, 2)
    return query_grads, total[0], total[1]


def solution(mesh):
    return jax.shard_map(
        local,
        mesh=mesh,
        in_specs=(
            P("view", "head", None),
            P("view", "head", None),
            P("view", "head", None),
            P("view", "head", None),
            P("head", None),
            P("view", None),
        ),
        out_specs=(P("view", "head", None), P("view", "head", None), P("view", "head", None)),
        check_vma=False,
    )
```

time: 301 us -> 118 us (0.39)
  waiting for transfers between devices: 137 us -> 22.1 us
  matrix products: 43.6 us -> 2.5 us
  other arithmetic: 40.8 us -> 2.17 us
  Pallas kernels: 0 us -> 36.1 us
  starting transfers between devices: 21.9 us -> 48.9 us
  local copies, waits for them, and re-layouts: 29.7 us -> 5.16 us
  loops' own time: 13.5 us -> 0 us
  between operations: 14.1 us -> 0.86 us
    ppermute x4 -> x13, waiting for transfers between devices: 136 us -> 22.1 us  [send(): return lax.ppermute(array, ('view', 'head'), pairs)]
    dot_general x25 -> x1, matrix products: 43.6 us -> 2.5 us  [local(): jnp.einsum('ij,vjt->vit', weight, gathered, preferred_element_type=single)]
    pallas_call x0 -> x3, Pallas kernels: none -> 36.1 us  [attn(): pl.pallas_call(attn_kernel, grid=(heads,), in_specs=[smem, smem, own, own...]
    ppermute x4 -> x13, starting transfers between devices: 21.8 us -> 48.9 us  [send(): return lax.ppermute(array, ('view', 'head'), pairs)]
    another operation x1 -> x0, loops' own time: 13.5 us -> none  [local(): query_grads, parts = lax.map(partial(query_side, with_parts=True), indices)]
    dynamic_update_slice x4 -> x0, other arithmetic: 10.6 us -> none  [local(): query_grads, parts = lax.map(partial(query_side, with_parts=True), indices)]
    squeeze x1, local copies, waits for them, and re-layouts: 11 us -> 1.14 us  [local(): return (query_grads, total[0], total[1])]
    slice x6 -> x2, local copies, waits for them, and re-layouts: 8.99 us -> 0.22 us  [local(): mine = own[:, :, first * DH:(first + heads) * DH]]
  transfers between devices with their start and end apart: 5 -> 13, of which waited for: 5 -> 4; matrix products, arithmetic and copies ran while one was open for 2% -> 6% of each run, Pallas kernels for 0% -> 31%
where the time goes in v2:
time: 118 us
  starting transfers between devices  48.9 us (41%)
  Pallas kernels  36.1 us (31%)
  waiting for transfers between devices  22.1 us (19%)
  local copies, waits for them, and re-layouts  5.16 us (4%)
  matrix products  2.5 us (2%)
  other arithmetic  2.17 us (2%)
    ppermute x13, starting transfers between devices, send(): return lax.ppermute(array, ('view', 'head'), pairs)  48.9 us
    pallas_call x3, Pallas kernels, attn(): pl.pallas_call(attn_kernel, grid=(heads,), in_specs=[smem, smem, own, own...  36.1 us
    ppermute x13, waiting for transfers between devices, send(): return lax.ppermute(array, ('view', 'head'), pairs)  22.1 us
    dot_general x1, matrix products, local(): jnp.einsum('ij,vjt->vit', weight, gathered, preferred_element_type=single)  2.5 us
  transfers between devices with their start and end apart: 13, of which 4 were waited for; matrix products, arithmetic and copies ran while one was open for 6% of the time, Pallas kernels for 31%

profile of v2, /device:TPU:1, one launch (start us, length us, event | category | flops | bytes accessed | tf_op | source)
XLA Modules:
  0.0 117.8 jit_solution(3556559151137175521)
XLA Ops:
  0.6 0.0 copy-start.4
  0.6 2.1 %collective-permute-start.1 = (bf16[4,320,256]{2,1,0:T(8,128)(2,1)}, bf16[4,320,256]{2,1,0:T(8,128)(2,1)}, u32[]{:S(2)}, u32[]{:S(2)}) collective-permute-start(bf16[4,320,256]{2,1,0:T(8,128)(2,1)} %param.21), channel_id=1, source_target_pairs={{0,2},{1,3},{2,0},{3,1},{4,6},{5,7},{6,4},{7,5},{8,10},{9,11},{10,... | collective-permute-start | bytes 1966088 | tf_op jit(solution)/shard_map/beside/ppermute | solution.py:187
  2.8 1.3 %collective-permute-start = (bf16[4,320,256]{2,1,0:T(8,128)(2,1)}, bf16[4,320,256]{2,1,0:T(8,128)(2,1)}, u32[]{:S(2)}, u32[]{:S(2)}) collective-permute-start(bf16[4,320,256]{2,1,0:T(8,128)(2,1)} %param.21), channel_id=1, source_target_pairs={{0,1},{1,0},{2,3},{3,2},{4,5},{5,4},{6,7},{7,6},{8,9},{9,8},{10,11... | collective-permute-start | bytes 1966088 | tf_op jit(solution)/shard_map/twin/ppermute | solution.py:187
  4.1 1.1 slice_bitcast_fusion.4
  5.1 0.0 copy-start
  5.2 0.0 copy-start.1
  5.2 1.0 fusion.17
  6.1 2.1 %collective-permute-start.3 = (bf16[2,3,128,256]{3,2,1,0:T(8,128)(2,1)}, bf16[2,3,128,256]{3,2,1,0:T(8,128)(2,1)S(1)}, u32[]{:S(2)}, u32[]{:S(2)}) collective-permute-start(bf16[2,3,128,256]{3,2,1,0:T(8,128)(2,1)} %get-tuple-element.136), channel_id=1, source_target_pairs={{0,4},{1,5},{2,6},{3,7},{4,0},{5,1},{6,2},{7,3},{8,12},{9,13},{10,... | collective-permute-start | bytes 1179656 | tf_op jit(solution)/shard_map/in_near_0/ppermute | solution.py:187
  8.2 8.3 %collective-permute-start.4 = (bf16[2,3,128,256]{3,2,1,0:T(8,128)(2,1)}, bf16[2,3,128,256]{3,2,1,0:T(8,128)(2,1)S(1)}, u32[]{:S(2)}, u32[]{:S(2)}) collective-permute-start(bf16[2,3,128,256]{3,2,1,0:T(8,128)(2,1)} %get-tuple-element.135), channel_id=1, source_target_pairs={{0,252},{1,253},{2,254},{3,255},{4,8},{5,9},{6,10},{7,11},{8,4},{9... | collective-permute-start | bytes 1179656 | tf_op jit(solution)/shard_map/in_far_0/ppermute | solution.py:187
  16.5 8.1 %collective-permute-done.1 = bf16[4,320,256]{2,1,0:T(8,128)(2,1)} collective-permute-done((bf16[4,320,256]{2,1,0:T(8,128)(2,1)}, bf16[4,320,256]{2,1,0:T(8,128)(2,1)}, u32[]{:S(2)}, u32[]{:S(2)}) %collective-permute-start.1) | collective-permute-done | bytes 655392 | tf_op jit(solution)/shard_map/beside/ppermute | solution.py:187
  24.6 5.8 %collective-permute-start.2 = (bf16[4,320,256]{2,1,0:T(8,128)(2,1)}, bf16[4,320,256]{2,1,0:T(8,128)(2,1)}, u32[]{:S(2)}, u32[]{:S(2)}) collective-permute-start(bf16[4,320,256]{2,1,0:T(8,128)(2,1)} %collective-permute-done.1), channel_id=1, source_target_pairs={{0,1},{1,0},{2,3},{3,2},{4,5},{5,4},{6,7},{7,6},{8,9},{9,8},{10,11... | collective-permute-start | bytes 1966088 | tf_op jit(solution)/shard_map/across/ppermute | solution.py:187
  30.4 0.0 copy-done.4
  30.4 1.2 %constant_dynamic-slice_fusion.2 = (bf16[320,320]{1,0:T(8,128)(2,1)S(1)}, bf16[320,320]{1,0:T(8,128)(2,1)S(1)}, bf16[320,320]{1,0:T(8,128)(2,1)}, bf16[320,320]{1,0:T(8,128)(2,1)}) fusion(bf16[320,1280]{1,0:T(8,128)(2,1)S(1)} %copy-done.4, s32[]{:T(128)S(6)} %select_n.63, s32[]{:T(128)S(6)} %select_n.61, s32[]{:T(128)S(6)} %select_n.60, s32[]{:T(128)S(6)} %select_n.62), kind=kLoop, calls=%fused_computation.36 | loop fusion | bytes 1638416 | tf_op jit(solution)/shard_map/dynamic_slice | solution.py:244
  31.6 1.4 %concatenate.22 = bf16[320,1280]{1,0:T(8,128)(2,1)S(1)} concatenate(bf16[320,320]{1,0:T(8,128)(2,1)} %get-tuple-element.131, bf16[320,320]{1,0:T(8,128)(2,1)S(1)} %get-tuple-element.130, bf16[320,320]{1,0:T(8,128)(2,1)} %get-tuple-element.132, bf16[320,320]{1,0:T(8,128)(2,1)S(1)} %get-tuple-element.129), dimensions={1} | concatenate | bytes 1638400 | tf_op jit(solution)/shard_map/concatenate | solution.py:243
  33.0 0.0 copy-done
  33.0 0.0 copy-done.1
  33.0 0.0 copy-start.5
  33.0 0.1 slice_bitcast_fusion.2
  33.1 0.1 pad_maximum_fusion.1
  33.1 0.1 constant_dynamic-slice_fusion
  33.2 1.0 collective-permute-start.5
  34.3 0.0 collective-permute-done
  34.3 0.0 copy-start.2
  34.3 0.0 copy-start.3
  34.3 8.2 %collective-permute-start.6 = (bf16[2,3,192,256]{3,2,1,0:T(8,128)(2,1)S(1)}, bf16[2,3,192,256]{3,2,1,0:T(8,128)(2,1)S(1)}, u32[]{:S(2)}, u32[]{:S(2)}) collective-permute-start(bf16[2,3,192,256]{3,2,1,0:T(8,128)(2,1)S(1)} %get-tuple-element.133), channel_id=1, source_target_pairs={{0,252},{1,253},{2,254},{3,255},{4,8},{5,9},{6,10},{7,11},{8,4},{9... | collective-permute-start | bytes 1769480 | tf_op jit(solution)/shard_map/in_far_2/ppermute | solution.py:187
  42.5 0.0 collective-permute-done.2
  42.5 0.0 copy-done.5
  42.5 2.5 %fusion.11.g_ref = bf16[4,320,256]{2,1,0:T(8,128)(2,1)S(1)} fusion(bf16[4,320,256]{2,1,0:T(8,128)(2,1)} %collective-permute-done.2, bf16[4,320,256]{2,1,0:T(8,128)(2,1)} %collective-permute-done.1, bf16[4,320,256]{2,1,0:T(8,128)(2,1)} %collective-permute-done, bf16[4,320,256]{2,1,0:T(8,128)(2,1)S(1)} %copy-done.5, bf16[320,1280]{1,0:T(8,128)(2,1)S(1)} %concatenate.22), kind=kOutput, calls=%fused_computation.10 | convolution fusion | flops 849674240 | bytes 4096000 | tf_op jit(solution)/shard_map/ij,vjt->vit/dot_general | solution.py:247
  45.0 0.0 collective-permute-done.3.near_ref
  45.0 0.0 collective-permute-done.4.far_ref
  45.0 0.0 copy-done.2
  45.0 0.0 copy-done.3
  45.0 14.3 %shard_map.85 = (bf16[4,320,256]{2,1,0:T(8,128)(2,1)}, f32[2,4,320,256]{3,2,1,0:T(8,128)S(1)}, bf16[2,3,128,256]{3,2,1,0:T(8,128)(2,1)S(1)}, bf16[2,3,128,256]{3,2,1,0:T(8,128)(2,1)S(1)}) custom-call(s32[4,7]{1,0:T(4,128)S(1)} %copy-done.3, s32[1]{0:T(128)} %bitcast.col_ref, bf16[4,320,256]{2,1,0:T(8,128)(2,1)S(1)} %copy-done.2, ...), custom_call_target="tpu_custom_call" | custom-call | flops 9395240960 | bytes 8388608 | tf_op jit(solution)/shard_map/pallas_call | solution.py:150
  59.3 3.2 %collective-permute-done.5.near_ref = bf16[2,3,192,256]{3,2,1,0:T(8,128)(2,1)S(1)} collective-permute-done((bf16[2,3,192,256]{3,2,1,0:T(8,128)(2,1)S(1)}, bf16[2,3,192,256]{3,2,1,0:T(8,128)(2,1)S(1)}, u32[]{:S(2)}, u32[]{:S(2)}) %collective-permute-start.5) | collective-permute-done | bytes 589856 | tf_op jit(solution)/shard_map/in_near_2/ppermute | solution.py:187
  62.5 0.0 collective-permute-done.6.far_ref
  62.5 0.9 collective-permute-start.7
  63.4 9.0 %collective-permute-start.8 = (bf16[2,3,128,256]{3,2,1,0:T(8,128)(2,1)S(1)}, bf16[2,3,128,256]{3,2,1,0:T(8,128)(2,1)S(1)}, u32[]{:S(2)}, u32[]{:S(2)}) collective-permute-start(bf16[2,3,128,256]{3,2,1,0:T(8,128)(2,1)S(1)} %get-tuple-element.104), channel_id=1, source_target_pairs={{0,252},{1,253},{2,254},{3,255},{4,8},{5,9},{6,10},{7,11},{8,4},{9... | collective-permute-start | bytes 1179656 | tf_op jit(solution)/shard_map/out_far_0/ppermute | solution.py:187
  72.4 14.3 %shard_map.86 = (bf16[4,320,256]{2,1,0:T(8,128)(2,1)}, f32[2,4,320,256]{3,2,1,0:T(8,128)S(1)}, bf16[2,3,128,256]{3,2,1,0:T(8,128)(2,1)S(1)}, bf16[2,3,128,256]{3,2,1,0:T(8,128)(2,1)S(1)}) custom-call(s32[4,7]{1,0:T(4,128)S(1)} %copy-done.3, s32[1]{0:T(128)} %bitcast.col_ref, ...), custom_call_target="tpu_custom_call", output_to_operand_aliasing={{0}: (8, {}), {1}: (9, {})} | custom-call | flops 9395240960 | bytes 8388608 | tf_op jit(solution)/shard_map/pallas_call | solution.py:150
  86.7 0.0 collective-permute-start.10
  86.7 0.0 collective-permute-start.9
  86.7 0.0 collective-permute-done.7
  86.7 0.0 collective-permute-done.8
  86.7 7.6 %shard_map.87 = (bf16[4,320,256]{2,1,0:T(8,128)(2,1)}, f32[2,4,320,256]{3,2,1,0:T(8,128)S(1)}, bf16[2,3,64,256]{3,2,1,0:T(8,128)(2,1)S(1)}, bf16[2,3,64,256]{3,2,1,0:T(8,128)(2,1)S(1)}) custom-call(s32[4,7]{1,0:T(4,128)S(1)} %copy-done.3, s32[1]{0:T(128)} %bitcast.col_ref, ...), custom_call_target="tpu_custom_call", output_to_operand_aliasing={{0}: (8, {}), {1}: (9, {})} | custom-call | flops 4697620480 | bytes 4194304 | tf_op jit(solution)/shard_map/pallas_call | solution.py:150
  94.3 3.0 %collective-permute-start.11 = (bf16[2,3,64,256]{3,2,1,0:T(8,128)(2,1)S(1)}, bf16[2,3,64,256]{3,2,1,0:T(8,128)(2,1)S(1)}, u32[]{:S(2)}, u32[]{:S(2)}) collective-permute-start(bf16[2,3,64,256]{3,2,1,0:T(8,128)(2,1)S(1)} %get-tuple-element.117), channel_id=1, source_target_pairs={{0,4},{1,5},{2,6},{3,7},{4,0},{5,1},{6,2},{7,3},{8,12},{9,13},{10,... | collective-permute-start | bytes 589832 | tf_op jit(solution)/shard_map/out_near_4/ppermute | solution.py:187
  97.3 7.2 %collective-permute-start.12 = (bf16[2,3,64,256]{3,2,1,0:T(8,128)(2,1)S(1)}, bf16[2,3,64,256]{3,2,1,0:T(8,128)(2,1)S(1)}, u32[]{:S(2)}, u32[]{:S(2)}) collective-permute-start(bf16[2,3,64,256]{3,2,1,0:T(8,128)(2,1)S(1)} %get-tuple-element.118), channel_id=1, source_target_pairs={{0,252},{1,253},{2,254},{3,255},{4,8},{5,9},{6,10},{7,11},{8,4},{9... | collective-permute-start | bytes 589832 | tf_op jit(solution)/shard_map/out_far_4/ppermute | solution.py:187
  104.5 0.2 fusion.21
  104.7 0.0 collective-permute-done.10
  104.7 6.5 %collective-permute-done.9 = bf16[2,3,128,256]{3,2,1,0:T(8,128)(2,1)S(1)} collective-permute-done((bf16[2,3,128,256]{3,2,1,0:T(8,128)(2,1)S(1)}, bf16[2,3,128,256]{3,2,1,0:T(8,128)(2,1)S(1)}, u32[]{:S(2)}, u32[]{:S(2)}) %collective-permute-start.9) | collective-permute-done | bytes 393248 | tf_op jit(solution)/shard_map/out_near_2/ppermute | solution.py:187
  111.2 4.2 %collective-permute-done.11 = bf16[2,3,64,256]{3,2,1,0:T(8,128)(2,1)S(1)} collective-permute-done((bf16[2,3,64,256]{3,2,1,0:T(8,128)(2,1)S(1)}, bf16[2,3,64,256]{3,2,1,0:T(8,128)(2,1)S(1)}, u32[]{:S(2)}, u32[]{:S(2)}) %collective-permute-start.11) | collective-permute-done | bytes 196640 | tf_op jit(solution)/shard_map/out_near_4/ppermute | solution.py:187
  115.4 0.0 collective-permute-done.12
  115.5 0.2 add_dynamic-update-slice_fusion.1
  115.7 0.3 fusion.16
  115.9 0.1 convert_element_type.36
  116.0 0.3 fusion.15
  116.3 0.1 convert_element_type.39
  116.3 0.1 add_dynamic-update-slice_fusion.2
  116.4 0.1 fusion.19
  116.6 0.1 pad_maximum_fusion
  116.6 1.1 slice_bitcast_fusion
  (2 shorter events, 0.1 us)
Async XLA Ops:
  0.6 29.8 %copy-start.4 = (bf16[320,1280]{1,0:T(8,128)(2,1)S(1)}, bf16[320,1280]{1,0:T(8,128)(2,1)}, u32[]{:S(2)}) copy-start(bf16[320,1280]{1,0:T(8,128)(2,1)} %param.22) | copy-start | bytes 2457604
  0.6 24.0 %collective-permute-start.1 = (bf16[4,320,256]{2,1,0:T(8,128)(2,1)}, bf16[4,320,256]{2,1,0:T(8,128)(2,1)}, u32[]{:S(2)}, u32[]{:S(2)}) collective-permute-start(bf16[4,320,256]{2,1,0:T(8,128)(2,1)} %param.21), channel_id=1, source_target_pairs={{0,2},{1,3},{2,0},{3,1},{4,6},{5,7},{6,4},{7,5},{8,10},{9,11},{10,... | collective-permute-start | bytes 1966088 | tf_op jit(solution)/shard_map/beside/ppermute | solution.py:187
  2.8 31.5 %collective-permute-start = (bf16[4,320,256]{2,1,0:T(8,128)(2,1)}, bf16[4,320,256]{2,1,0:T(8,128)(2,1)}, u32[]{:S(2)}, u32[]{:S(2)}) collective-permute-start(bf16[4,320,256]{2,1,0:T(8,128)(2,1)} %param.21), channel_id=1, source_target_pairs={{0,1},{1,0},{2,3},{3,2},{4,5},{5,4},{6,7},{7,6},{8,9},{9,8},{10,11... | collective-permute-start | bytes 1966088 | tf_op jit(solution)/shard_map/twin/ppermute | solution.py:187
  5.1 27.8 %copy-start = (bf16[4,320,256]{2,1,0:T(8,128)(2,1)S(1)}, bf16[4,320,256]{2,1,0:T(8,128)(2,1)}, u32[]{:S(2)}) copy-start(bf16[4,320,256]{2,1,0:T(8,128)(2,1)} %k_ref.5) | copy-start | bytes 1966084
  5.2 27.8 %copy-start.1 = (bf16[4,320,256]{2,1,0:T(8,128)(2,1)S(1)}, bf16[4,320,256]{2,1,0:T(8,128)(2,1)}, u32[]{:S(2)}) copy-start(bf16[4,320,256]{2,1,0:T(8,128)(2,1)} %v_ref.5) | copy-start | bytes 1966084
  6.1 38.9 %collective-permute-start.3 = (bf16[2,3,128,256]{3,2,1,0:T(8,128)(2,1)}, bf16[2,3,128,256]{3,2,1,0:T(8,128)(2,1)S(1)}, u32[]{:S(2)}, u32[]{:S(2)}) collective-permute-start(bf16[2,3,128,256]{3,2,1,0:T(8,128)(2,1)} %get-tuple-element.136), channel_id=1, source_target_pairs={{0,4},{1,5},{2,6},{3,7},{4,0},{5,1},{6,2},{7,3},{8,12},{9,13},{10,... | collective-permute-start | bytes 1179656 | tf_op jit(solution)/shard_map/in_near_0/ppermute | solution.py:187
  8.2 36.8 %collective-permute-start.4 = (bf16[2,3,128,256]{3,2,1,0:T(8,128)(2,1)}, bf16[2,3,128,256]{3,2,1,0:T(8,128)(2,1)S(1)}, u32[]{:S(2)}, u32[]{:S(2)}) collective-permute-start(bf16[2,3,128,256]{3,2,1,0:T(8,128)(2,1)} %get-tuple-element.135), channel_id=1, source_target_pairs={{0,252},{1,253},{2,254},{3,255},{4,8},{5,9},{6,10},{7,11},{8,4},{9... | collective-permute-start | bytes 1179656 | tf_op jit(solution)/shard_map/in_far_0/ppermute | solution.py:187
  24.6 17.9 %collective-permute-start.2 = (bf16[4,320,256]{2,1,0:T(8,128)(2,1)}, bf16[4,320,256]{2,1,0:T(8,128)(2,1)}, u32[]{:S(2)}, u32[]{:S(2)}) collective-permute-start(bf16[4,320,256]{2,1,0:T(8,128)(2,1)} %collective-permute-done.1), channel_id=1, source_target_pairs={{0,1},{1,0},{2,3},{3,2},{4,5},{5,4},{6,7},{7,6},{8,9},{9,8},{10,11... | collective-permute-start | bytes 1966088 | tf_op jit(solution)/shard_map/across/ppermute | solution.py:187
  33.0 9.5 %copy-start.5 = (bf16[4,320,256]{2,1,0:T(8,128)(2,1)S(1)}, bf16[4,320,256]{2,1,0:T(8,128)(2,1)}, u32[]{:S(2)}) copy-start(bf16[4,320,256]{2,1,0:T(8,128)(2,1)} %param.21) | copy-start | bytes 1966084
  33.2 29.3 %collective-permute-start.5 = (bf16[2,3,192,256]{3,2,1,0:T(8,128)(2,1)S(1)}, bf16[2,3,192,256]{3,2,1,0:T(8,128)(2,1)S(1)}, u32[]{:S(2)}, u32[]{:S(2)}) collective-permute-start(bf16[2,3,192,256]{3,2,1,0:T(8,128)(2,1)S(1)} %get-tuple-element.134), channel_id=1, source_target_pairs={{0,4},{1,5},{2,6},{3,7},{4,0},{5,1},{6,2},{7,3},{8,12},{9,13},{10,... | collective-permute-start | bytes 1769480 | tf_op jit(solution)/shard_map/in_near_2/ppermute | solution.py:187
  34.3 10.7 %copy-start.2 = (bf16[4,320,256]{2,1,0:T(8,128)(2,1)S(1)}, bf16[4,320,256]{2,1,0:T(8,128)(2,1)}, u32[]{:S(2)}) copy-start(bf16[4,320,256]{2,1,0:T(8,128)(2,1)} %q_ref.5) | copy-start | bytes 1966084
  34.3 10.7 %copy-start.3 = (s32[4,7]{1,0:T(4,128)S(1)}, s32[4,7]{1,0:T(4,128)}, u32[]{:S(2)}) copy-start(s32[4,7]{1,0:T(4,128)} %vis_ref.5) | copy-start | bytes 340
  34.3 28.2 %collective-permute-start.6 = (bf16[2,3,192,256]{3,2,1,0:T(8,128)(2,1)S(1)}, bf16[2,3,192,256]{3,2,1,0:T(8,128)(2,1)S(1)}, u32[]{:S(2)}, u32[]{:S(2)}) collective-permute-start(bf16[2,3,192,256]{3,2,1,0:T(8,128)(2,1)S(1)} %get-tuple-element.133), channel_id=1, source_target_pairs={{0,252},{1,253},{2,254},{3,255},{4,8},{5,9},{6,10},{7,11},{8,4},{9... | collective-permute-start | bytes 1769480 | tf_op jit(solution)/shard_map/in_far_2/ppermute | solution.py:187
  62.5 24.2 %collective-permute-start.7 = (bf16[2,3,128,256]{3,2,1,0:T(8,128)(2,1)S(1)}, bf16[2,3,128,256]{3,2,1,0:T(8,128)(2,1)S(1)}, u32[]{:S(2)}, u32[]{:S(2)}) collective-permute-start(bf16[2,3,128,256]{3,2,1,0:T(8,128)(2,1)S(1)} %get-tuple-element.103), channel_id=1, source_target_pairs={{0,4},{1,5},{2,6},{3,7},{4,0},{5,1},{6,2},{7,3},{8,12},{9,13},{10,... | collective-permute-start | bytes 1179656 | tf_op jit(solution)/shard_map/out_near_0/ppermute | solution.py:187
  63.4 23.3 %collective-permute-start.8 = (bf16[2,3,128,256]{3,2,1,0:T(8,128)(2,1)S(1)}, bf16[2,3,128,256]{3,2,1,0:T(8,128)(2,1)S(1)}, u32[]{:S(2)}, u32[]{:S(2)}) collective-permute-start(bf16[2,3,128,256]{3,2,1,0:T(8,128)(2,1)S(1)} %get-tuple-element.104), channel_id=1, source_target_pairs={{0,252},{1,253},{2,254},{3,255},{4,8},{5,9},{6,10},{7,11},{8,4},{9... | collective-permute-start | bytes 1179656 | tf_op jit(solution)/shard_map/out_far_0/ppermute | solution.py:187
  86.7 18.0 %collective-permute-start.10 = (bf16[2,3,128,256]{3,2,1,0:T(8,128)(2,1)S(1)}, bf16[2,3,128,256]{3,2,1,0:T(8,128)(2,1)S(1)}, u32[]{:S(2)}, u32[]{:S(2)}) collective-permute-start(bf16[2,3,128,256]{3,2,1,0:T(8,128)(2,1)S(1)} %get-tuple-element.116), channel_id=1, source_target_pairs={{0,252},{1,253},{2,254},{3,255},{4,8},{5,9},{6,10},{7,11},{8,4},{9... | collective-permute-start | bytes 1179656 | tf_op jit(solution)/shard_map/out_far_2/ppermute | solution.py:187
  86.7 24.6 %collective-permute-start.9 = (bf16[2,3,128,256]{3,2,1,0:T(8,128)(2,1)S(1)}, bf16[2,3,128,256]{3,2,1,0:T(8,128)(2,1)S(1)}, u32[]{:S(2)}, u32[]{:S(2)}) collective-permute-start(bf16[2,3,128,256]{3,2,1,0:T(8,128)(2,1)S(1)} %get-tuple-element.115), channel_id=1, source_target_pairs={{0,4},{1,5},{2,6},{3,7},{4,0},{5,1},{6,2},{7,3},{8,12},{9,13},{10,... | collective-permute-start | bytes 1179656 | tf_op jit(solution)/shard_map/out_near_2/ppermute | solution.py:187
  94.3 21.1 %collective-permute-start.11 = (bf16[2,3,64,256]{3,2,1,0:T(8,128)(2,1)S(1)}, bf16[2,3,64,256]{3,2,1,0:T(8,128)(2,1)S(1)}, u32[]{:S(2)}, u32[]{:S(2)}) collective-permute-start(bf16[2,3,64,256]{3,2,1,0:T(8,128)(2,1)S(1)} %get-tuple-element.117), channel_id=1, source_target_pairs={{0,4},{1,5},{2,6},{3,7},{4,0},{5,1},{6,2},{7,3},{8,12},{9,13},{10,... | collective-permute-start | bytes 589832 | tf_op jit(solution)/shard_map/out_near_4/ppermute | solution.py:187
  97.3 18.2 %collective-permute-start.12 = (bf16[2,3,64,256]{3,2,1,0:T(8,128)(2,1)S(1)}, bf16[2,3,64,256]{3,2,1,0:T(8,128)(2,1)S(1)}, u32[]{:S(2)}, u32[]{:S(2)}) collective-permute-start(bf16[2,3,64,256]{3,2,1,0:T(8,128)(2,1)S(1)} %get-tuple-element.118), channel_id=1, source_target_pairs={{0,252},{1,253},{2,254},{3,255},{4,8},{5,9},{6,10},{7,11},{8,4},{9... | collective-permute-start | bytes 589832 | tf_op jit(solution)/shard_map/out_far_4/ppermute | solution.py:187

commit v3 on v2

--- a/solution.py
+++ b/solution.py
@@ -8,7 +8,7 @@
 DH = 64
 R = 3
 STRIP = 64
-GROUPS = ((2, False), (3, False))
+GROUPS = ((2, True), (2, False), (1, False))
 PARTS = ((2, False), (2, False), (1, False))
 
 

time: 118 us -> 115 us (0.975)
  starting transfers between devices: 48.9 us -> 38 us
  waiting for transfers between devices: 22.1 us -> 27.7 us
    ppermute x13 -> x15, starting transfers between devices: 48.9 us -> 38 us  [send(): return lax.ppermute(array, ('view', 'head'), pairs)]
    ppermute x13 -> x15, waiting for transfers between devices: 22.1 us -> 27.7 us  [send(): return lax.ppermute(array, ('view', 'head'), pairs)]
  transfers between devices with their start and end apart: 13 -> 15, of which waited for: 4 -> 5; matrix products, arithmetic and copies ran while one was open for 6% -> 8% of each run, Pallas kernels for 31% -> 32%
where the time goes in v3:
time: 115 us; the launch traced here: 114 us
  starting transfers between devices  38 us (33%)
  Pallas kernels  36.1 us (31%)
  waiting for transfers between devices  27.7 us (24%)
  local copies, waits for them, and re-layouts  6.09 us (5%)
  other arithmetic  3.03 us (3%)
  matrix products  2.5 us (2%)
    ppermute x15, starting transfers between devices, send(): return lax.ppermute(array, ('view', 'head'), pairs)  38 us
    pallas_call x3, Pallas kernels, attn(): pl.pallas_call(attn_kernel, grid=(heads,), in_specs=[smem, smem, own, own...  36.1 us
    ppermute x15, waiting for transfers between devices, send(): return lax.ppermute(array, ('view', 'head'), pairs)  27.7 us
    dot_general x1, matrix products, local(): jnp.einsum('ij,vjt->vit', weight, gathered, preferred_element_type=single)  2.5 us
  transfers between devices with their start and end apart: 15, of which 5 were waited for; matrix products, arithmetic and copies ran while one was open for 8% of the time, Pallas kernels for 32%

profile of v3, /device:TPU:1, one launch (start us, length us, event | category | flops | bytes accessed | tf_op | source)
XLA Modules:
  0.0 114.3 jit_solution(11301661962981523634)
XLA Ops:
  0.6 0.0 copy-start
  0.6 0.0 copy-start.1
  0.7 0.0 copy-start.4
  0.7 2.1 %collective-permute-start.1 = (bf16[4,320,256]{2,1,0:T(8,128)(2,1)}, bf16[4,320,256]{2,1,0:T(8,128)(2,1)}, u32[]{:S(2)}, u32[]{:S(2)}) collective-permute-start(bf16[4,320,256]{2,1,0:T(8,128)(2,1)} %param.21), channel_id=1, source_target_pairs={{0,2},{1,3},{2,0},{3,1},{4,6},{5,7},{6,4},{7,5},{8,10},{9,11},{10,... | collective-permute-start | bytes 1966088 | tf_op jit(solution)/shard_map/beside/ppermute | solution.py:187
  2.8 1.3 %collective-permute-start = (bf16[4,320,256]{2,1,0:T(8,128)(2,1)}, bf16[4,320,256]{2,1,0:T(8,128)(2,1)}, u32[]{:S(2)}, u32[]{:S(2)}) collective-permute-start(bf16[4,320,256]{2,1,0:T(8,128)(2,1)} %param.21), channel_id=1, source_target_pairs={{0,1},{1,0},{2,3},{3,2},{4,5},{5,4},{6,7},{7,6},{8,9},{9,8},{10,11... | collective-permute-start | bytes 1966088 | tf_op jit(solution)/shard_map/twin/ppermute | solution.py:187
  4.1 1.3 %slice_bitcast_fusion.2 = (bf16[1,4,128,256]{3,2,1,0:T(8,128)(2,1)S(1)}, bf16[1,4,128,256]{3,2,1,0:T(8,128)(2,1)S(1)}, bf16[1,4,128,256]{3,2,1,0:T(8,128)(2,1)S(1)}, bf16[1,4,128,256]{3,2,1,0:T(8,128)(2,1)S(1)}) fusion(bf16[4,320,256]{2,1,0:T(8,128)(2,1)} %v_ref.5, bf16[4,320,256]{2,1,0:T(8,128)(2,1)} %k_ref.5), kind=kLoop, calls=%fused_computation.26 | loop fusion | bytes 2097152 | tf_op jit(solution)/shard_map/stack | solution.py:224
  5.4 0.8 pad_maximum_fusion.1
  6.2 2.1 %collective-permute-start.4 = (bf16[2,4,128,256]{3,2,1,0:T(8,128)(2,1)}, bf16[2,4,128,256]{3,2,1,0:T(8,128)(2,1)S(1)}, u32[]{:S(2)}, u32[]{:S(2)}) collective-permute-start(bf16[2,4,128,256]{3,2,1,0:T(8,128)(2,1)} %pad_maximum_fusion.1), channel_id=1, source_target_pairs={{0,4},{1,5},{2,6},{3,7},{4,0},{5,1},{6,2},{7,3},{8,12},{9,13},{10,... | collective-permute-start | bytes 1572872 | tf_op jit(solution)/shard_map/in_near_0/ppermute | solution.py:187
  8.3 0.0 copy-done
  8.3 0.0 copy-done.1
  8.3 0.7 slice_bitcast_fusion.6
  9.0 7.2 %collective-permute-done.1 = bf16[4,320,256]{2,1,0:T(8,128)(2,1)} collective-permute-done((bf16[4,320,256]{2,1,0:T(8,128)(2,1)}, bf16[4,320,256]{2,1,0:T(8,128)(2,1)}, u32[]{:S(2)}, u32[]{:S(2)}) %collective-permute-start.1) | collective-permute-done | bytes 655392 | tf_op jit(solution)/shard_map/beside/ppermute | solution.py:187
  16.2 5.8 %collective-permute-start.2 = (bf16[4,320,256]{2,1,0:T(8,128)(2,1)}, bf16[4,320,256]{2,1,0:T(8,128)(2,1)}, u32[]{:S(2)}, u32[]{:S(2)}) collective-permute-start(bf16[4,320,256]{2,1,0:T(8,128)(2,1)} %collective-permute-done.1), channel_id=1, source_target_pairs={{0,1},{1,0},{2,3},{3,2},{4,5},{5,4},{6,7},{7,6},{8,9},{9,8},{10,11... | collective-permute-start | bytes 1966088 | tf_op jit(solution)/shard_map/across/ppermute | solution.py:187
  22.0 0.0 copy-done.4
  22.0 1.3 %constant_dynamic-slice_fusion.5 = (bf16[320,320]{1,0:T(8,128)(2,1)S(1)}, bf16[320,320]{1,0:T(8,128)(2,1)}, bf16[320,320]{1,0:T(8,128)(2,1)}, bf16[320,320]{1,0:T(8,128)(2,1)}) fusion(bf16[320,1280]{1,0:T(8,128)(2,1)S(1)} %copy-done.4, s32[]{:T(128)S(6)} %select_n.64, s32[]{:T(128)S(6)} %select_n.62, s32[]{:T(128)S(6)} %select_n.61, s32[]{:T(128)S(6)} %select_n.63), kind=kLoop, calls=%fused_computation.37 | loop fusion | bytes 1638416 | tf_op jit(solution)/shard_map/dynamic_slice | solution.py:244
  23.2 1.4 %concatenate.22 = bf16[320,1280]{1,0:T(8,128)(2,1)S(1)} concatenate(bf16[320,320]{1,0:T(8,128)(2,1)} %get-tuple-element.133, bf16[320,320]{1,0:T(8,128)(2,1)} %get-tuple-element.132, bf16[320,320]{1,0:T(8,128)(2,1)} %get-tuple-element.134, bf16[320,320]{1,0:T(8,128)(2,1)S(1)} %get-tuple-element.131), dimensions={1} | concatenate | bytes 1638400 | tf_op jit(solution)/shard_map/concatenate | solution.py:243
  24.7 0.0 copy-start.5
  24.7 1.0 pad_maximum_fusion.3
  25.7 0.1 pad_maximum_fusion.2
  25.8 5.1 %collective-permute-done.4.near_ref = bf16[2,4,128,256]{3,2,1,0:T(8,128)(2,1)S(1)} collective-permute-done((bf16[2,4,128,256]{3,2,1,0:T(8,128)(2,1)}, bf16[2,4,128,256]{3,2,1,0:T(8,128)(2,1)S(1)}, u32[]{:S(2)}, u32[]{:S(2)}) %collective-permute-start.4) | collective-permute-done | bytes 524320 | tf_op jit(solution)/shard_map/in_near_0/ppermute | solution.py:187
  30.8 1.7 %collective-permute-start.5 = (bf16[2,3,128,256]{3,2,1,0:T(8,128)(2,1)S(1)}, bf16[2,3,128,256]{3,2,1,0:T(8,128)(2,1)S(1)}, u32[]{:S(2)}, u32[]{:S(2)}) collective-permute-start(bf16[2,3,128,256]{3,2,1,0:T(8,128)(2,1)S(1)} %constant_dynamic-slice_fusion.3), channel_id=1, source_target_pairs={{0,8},{1,9},{2,10},{3,11},{4,252},{5,253},{6,254},{7,255},{8,16},{... | collective-permute-start | bytes 1179656 | tf_op jit(solution)/shard_map/in_far_0/ppermute | solution.py:187
  32.6 7.0 %collective-permute-start.3 = (bf16[2,3,64,256]{3,2,1,0:T(8,128)(2,1)S(1)}, bf16[2,3,64,256]{3,2,1,0:T(8,128)(2,1)S(1)}, u32[]{:S(2)}, u32[]{:S(2)}) collective-permute-start(bf16[2,3,64,256]{3,2,1,0:T(8,128)(2,1)S(1)} %get-tuple-element.142), channel_id=1, source_target_pairs={{0,4},{1,5},{2,6},{3,7},{4,0},{5,1},{6,2},{7,3},{8,12},{9,13},{10,... | collective-permute-start | bytes 589832 | tf_op jit(solution)/shard_map/in_near_4/ppermute | solution.py:187
  39.6 0.1 constant_dynamic-slice_fusion.1
  39.6 0.1 collective-permute-start.6
  39.8 0.0 collective-permute-done
  39.8 3.4 %collective-permute-start.7 = (bf16[2,3,128,256]{3,2,1,0:T(8,128)(2,1)S(1)}, bf16[2,3,128,256]{3,2,1,0:T(8,128)(2,1)S(1)}, u32[]{:S(2)}, u32[]{:S(2)}) collective-permute-start(bf16[2,3,128,256]{3,2,1,0:T(8,128)(2,1)S(1)} %get-tuple-element.139), channel_id=1, source_target_pairs={{0,252},{1,253},{2,254},{3,255},{4,8},{5,9},{6,10},{7,11},{8,4},{9... | collective-permute-start | bytes 1179656 | tf_op jit(solution)/shard_map/in_far_2/ppermute | solution.py:187
  43.2 0.0 collective-permute-done.2
  43.2 0.0 copy-start.2
  43.2 0.0 copy-start.3
  43.2 3.9 %collective-permute-start.10 = (bf16[2,3,64,256]{3,2,1,0:T(8,128)(2,1)S(1)}, bf16[2,3,64,256]{3,2,1,0:T(8,128)(2,1)S(1)}, u32[]{:S(2)}, u32[]{:S(2)}) collective-permute-start(bf16[2,3,64,256]{3,2,1,0:T(8,128)(2,1)S(1)} %get-tuple-element.141), channel_id=1, source_target_pairs={{0,252},{1,253},{2,254},{3,255},{4,8},{5,9},{6,10},{7,11},{8,4},{9... | collective-permute-start | bytes 589832 | tf_op jit(solution)/shard_map/in_far_4/ppermute | solution.py:187
  47.0 0.0 copy-done.5
  47.0 2.5 %fusion.11.g_ref = bf16[4,320,256]{2,1,0:T(8,128)(2,1)S(1)} fusion(bf16[4,320,256]{2,1,0:T(8,128)(2,1)} %collective-permute-done.2, bf16[4,320,256]{2,1,0:T(8,128)(2,1)} %collective-permute-done.1, bf16[4,320,256]{2,1,0:T(8,128)(2,1)} %collective-permute-done, bf16[4,320,256]{2,1,0:T(8,128)(2,1)S(1)} %copy-done.5, bf16[320,1280]{1,0:T(8,128)(2,1)S(1)} %concatenate.22), kind=kOutput, calls=%fused_computation.10 | convolution fusion | flops 849674240 | bytes 4096000 | tf_op jit(solution)/shard_map/ij,vjt->vit/dot_general | solution.py:247
  49.6 0.0 collective-permute-done.5.far_ref
  49.6 0.0 copy-done.2
  49.6 0.0 copy-done.3
  49.6 14.3 %shard_map.85 = (bf16[4,320,256]{2,1,0:T(8,128)(2,1)}, f32[2,4,320,256]{3,2,1,0:T(8,128)S(1)}, bf16[2,3,128,256]{3,2,1,0:T(8,128)(2,1)S(1)}, bf16[2,3,128,256]{3,2,1,0:T(8,128)(2,1)S(1)}) custom-call(s32[4,7]{1,0:T(4,128)S(1)} %copy-done.3, s32[1]{0:T(128)} %bitcast.col_ref, bf16[4,320,256]{2,1,0:T(8,128)(2,1)S(1)} %copy-done.2, ...), custom_call_target="tpu_custom_call" | custom-call | flops 9395240960 | bytes 8388608 | tf_op jit(solution)/shard_map/pallas_call | solution.py:150
  63.9 2.5 %collective-permute-done.6.near_ref = bf16[2,3,128,256]{3,2,1,0:T(8,128)(2,1)S(1)} collective-permute-done((bf16[2,3,128,256]{3,2,1,0:T(8,128)(2,1)S(1)}, bf16[2,3,128,256]{3,2,1,0:T(8,128)(2,1)S(1)}, u32[]{:S(2)}, u32[]{:S(2)}) %collective-permute-start.6) | collective-permute-done | bytes 393248 | tf_op jit(solution)/shard_map/in_near_2/ppermute | solution.py:187
  66.4 0.0 collective-permute-done.7.far_ref
  66.4 0.4 collective-permute-start.8
  66.7 2.5 %collective-permute-start.9 = (bf16[2,3,128,256]{3,2,1,0:T(8,128)(2,1)S(1)}, bf16[2,3,128,256]{3,2,1,0:T(8,128)(2,1)S(1)}, u32[]{:S(2)}, u32[]{:S(2)}) collective-permute-start(bf16[2,3,128,256]{3,2,1,0:T(8,128)(2,1)S(1)} %get-tuple-element.105), channel_id=1, source_target_pairs={{0,252},{1,253},{2,254},{3,255},{4,8},{5,9},{6,10},{7,11},{8,4},{9... | collective-permute-start | bytes 1179656 | tf_op jit(solution)/shard_map/out_far_0/ppermute | solution.py:187
  69.2 14.3 %shard_map.86 = (bf16[4,320,256]{2,1,0:T(8,128)(2,1)}, f32[2,4,320,256]{3,2,1,0:T(8,128)S(1)}, bf16[2,3,128,256]{3,2,1,0:T(8,128)(2,1)S(1)}, bf16[2,3,128,256]{3,2,1,0:T(8,128)(2,1)S(1)}) custom-call(s32[4,7]{1,0:T(4,128)S(1)} %copy-done.3, s32[1]{0:T(128)} %bitcast.col_ref, ...), custom_call_target="tpu_custom_call", output_to_operand_aliasing={{0}: (8, {}), {1}: (9, {})} | custom-call | flops 9395240960 | bytes 8388608 | tf_op jit(solution)/shard_map/pallas_call | solution.py:150
  83.5 0.1 collective-permute-start.11
  83.6 0.0 collective-permute-done.3.near_ref
  83.6 4.8 %collective-permute-start.12 = (bf16[2,3,128,256]{3,2,1,0:T(8,128)(2,1)S(1)}, bf16[2,3,128,256]{3,2,1,0:T(8,128)(2,1)S(1)}, u32[]{:S(2)}, u32[]{:S(2)}) collective-permute-start(bf16[2,3,128,256]{3,2,1,0:T(8,128)(2,1)S(1)} %get-tuple-element.118), channel_id=1, source_target_pairs={{0,252},{1,253},{2,254},{3,255},{4,8},{5,9},{6,10},{7,11},{8,4},{9... | collective-permute-start | bytes 1179656 | tf_op jit(solution)/shard_map/out_far_2/ppermute | solution.py:187
  88.4 0.0 collective-permute-done.8
  88.4 0.0 collective-permute-done.9
  88.4 0.0 collective-permute-done.10.far_ref
  88.4 7.6 %shard_map.87 = (bf16[4,320,256]{2,1,0:T(8,128)(2,1)}, f32[2,4,320,256]{3,2,1,0:T(8,128)S(1)}, bf16[2,3,64,256]{3,2,1,0:T(8,128)(2,1)S(1)}, bf16[2,3,64,256]{3,2,1,0:T(8,128)(2,1)S(1)}) custom-call(s32[4,7]{1,0:T(4,128)S(1)} %copy-done.3, s32[1]{0:T(128)} %bitcast.col_ref, ...), custom_call_target="tpu_custom_call", output_to_operand_aliasing={{0}: (8, {}), {1}: (9, {})} | custom-call | flops 4697620480 | bytes 4194304 | tf_op jit(solution)/shard_map/pallas_call | solution.py:150
  96.1 0.1 collective-permute-start.13
  96.2 2.7 %collective-permute-start.14 = (bf16[2,3,64,256]{3,2,1,0:T(8,128)(2,1)S(1)}, bf16[2,3,64,256]{3,2,1,0:T(8,128)(2,1)S(1)}, u32[]{:S(2)}, u32[]{:S(2)}) collective-permute-start(bf16[2,3,64,256]{3,2,1,0:T(8,128)(2,1)S(1)} %get-tuple-element.120), channel_id=1, source_target_pairs={{0,252},{1,253},{2,254},{3,255},{4,8},{5,9},{6,10},{7,11},{8,4},{9... | collective-permute-start | bytes 589832 | tf_op jit(solution)/shard_map/out_far_4/ppermute | solution.py:187
  98.9 0.1 fusion.19
  99.1 8.7 %collective-permute-done.11 = bf16[2,3,128,256]{3,2,1,0:T(8,128)(2,1)S(1)} collective-permute-done((bf16[2,3,128,256]{3,2,1,0:T(8,128)(2,1)S(1)}, bf16[2,3,128,256]{3,2,1,0:T(8,128)(2,1)S(1)}, u32[]{:S(2)}, u32[]{:S(2)}) %collective-permute-start.11) | collective-permute-done | bytes 393248 | tf_op jit(solution)/shard_map/out_near_2/ppermute | solution.py:187
  107.8 0.0 collective-permute-done.12
  107.8 4.2 %collective-permute-done.13 = bf16[2,3,64,256]{3,2,1,0:T(8,128)(2,1)S(1)} collective-permute-done((bf16[2,3,64,256]{3,2,1,0:T(8,128)(2,1)S(1)}, bf16[2,3,64,256]{3,2,1,0:T(8,128)(2,1)S(1)}, u32[]{:S(2)}, u32[]{:S(2)}) %collective-permute-start.13) | collective-permute-done | bytes 196640 | tf_op jit(solution)/shard_map/out_near_4/ppermute | solution.py:187
  112.0 0.0 collective-permute-done.14
  112.0 0.1 add_dynamic-update-slice_fusion.2
  112.1 0.1 fusion.17
  112.2 0.2 add_dynamic-update-slice_fusion.1
  112.5 0.3 fusion.15
  112.7 0.1 convert_element_type.39
  112.8 0.3 fusion.16
  113.0 0.1 convert_element_type.36
  113.1 0.1 pad_maximum_fusion
  113.2 1.1 slice_bitcast_fusion
  (4 shorter events, 0.1 us)
Async XLA Ops:
  0.6 7.7 %copy-start = (bf16[4,320,256]{2,1,0:T(8,128)(2,1)S(1)}, bf16[4,320,256]{2,1,0:T(8,128)(2,1)}, u32[]{:S(2)}) copy-start(bf16[4,320,256]{2,1,0:T(8,128)(2,1)} %k_ref.5) | copy-start | bytes 1966084
  0.6 7.7 %copy-start.1 = (bf16[4,320,256]{2,1,0:T(8,128)(2,1)S(1)}, bf16[4,320,256]{2,1,0:T(8,128)(2,1)}, u32[]{:S(2)}) copy-start(bf16[4,320,256]{2,1,0:T(8,128)(2,1)} %v_ref.5) | copy-start | bytes 1966084
  0.7 21.3 %copy-start.4 = (bf16[320,1280]{1,0:T(8,128)(2,1)S(1)}, bf16[320,1280]{1,0:T(8,128)(2,1)}, u32[]{:S(2)}) copy-start(bf16[320,1280]{1,0:T(8,128)(2,1)} %param.22) | copy-start | bytes 2457604
  0.7 15.5 %collective-permute-start.1 = (bf16[4,320,256]{2,1,0:T(8,128)(2,1)}, bf16[4,320,256]{2,1,0:T(8,128)(2,1)}, u32[]{:S(2)}, u32[]{:S(2)}) collective-permute-start(bf16[4,320,256]{2,1,0:T(8,128)(2,1)} %param.21), channel_id=1, source_target_pairs={{0,2},{1,3},{2,0},{3,1},{4,6},{5,7},{6,4},{7,5},{8,10},{9,11},{10,... | collective-permute-start | bytes 1966088 | tf_op jit(solution)/shard_map/beside/ppermute | solution.py:187
  2.8 37.0 %collective-permute-start = (bf16[4,320,256]{2,1,0:T(8,128)(2,1)}, bf16[4,320,256]{2,1,0:T(8,128)(2,1)}, u32[]{:S(2)}, u32[]{:S(2)}) collective-permute-start(bf16[4,320,256]{2,1,0:T(8,128)(2,1)} %param.21), channel_id=1, source_target_pairs={{0,1},{1,0},{2,3},{3,2},{4,5},{5,4},{6,7},{7,6},{8,9},{9,8},{10,11... | collective-permute-start | bytes 1966088 | tf_op jit(solution)/shard_map/twin/ppermute | solution.py:187
  6.2 24.6 %collective-permute-start.4 = (bf16[2,4,128,256]{3,2,1,0:T(8,128)(2,1)}, bf16[2,4,128,256]{3,2,1,0:T(8,128)(2,1)S(1)}, u32[]{:S(2)}, u32[]{:S(2)}) collective-permute-start(bf16[2,4,128,256]{3,2,1,0:T(8,128)(2,1)} %pad_maximum_fusion.1), channel_id=1, source_target_pairs={{0,4},{1,5},{2,6},{3,7},{4,0},{5,1},{6,2},{7,3},{8,12},{9,13},{10,... | collective-permute-start | bytes 1572872 | tf_op jit(solution)/shard_map/in_near_0/ppermute | solution.py:187
  16.2 26.9 %collective-permute-start.2 = (bf16[4,320,256]{2,1,0:T(8,128)(2,1)}, bf16[4,320,256]{2,1,0:T(8,128)(2,1)}, u32[]{:S(2)}, u32[]{:S(2)}) collective-permute-start(bf16[4,320,256]{2,1,0:T(8,128)(2,1)} %collective-permute-done.1), channel_id=1, source_target_pairs={{0,1},{1,0},{2,3},{3,2},{4,5},{5,4},{6,7},{7,6},{8,9},{9,8},{10,11... | collective-permute-start | bytes 1966088 | tf_op jit(solution)/shard_map/across/ppermute | solution.py:187
  24.7 22.4 %copy-start.5 = (bf16[4,320,256]{2,1,0:T(8,128)(2,1)S(1)}, bf16[4,320,256]{2,1,0:T(8,128)(2,1)}, u32[]{:S(2)}) copy-start(bf16[4,320,256]{2,1,0:T(8,128)(2,1)} %param.21) | copy-start | bytes 1966084
  30.8 18.7 %collective-permute-start.5 = (bf16[2,3,128,256]{3,2,1,0:T(8,128)(2,1)S(1)}, bf16[2,3,128,256]{3,2,1,0:T(8,128)(2,1)S(1)}, u32[]{:S(2)}, u32[]{:S(2)}) collective-permute-start(bf16[2,3,128,256]{3,2,1,0:T(8,128)(2,1)S(1)} %constant_dynamic-slice_fusion.3), channel_id=1, source_target_pairs={{0,8},{1,9},{2,10},{3,11},{4,252},{5,253},{6,254},{7,255},{8,16},{... | collective-permute-start | bytes 1179656 | tf_op jit(solution)/shard_map/in_far_0/ppermute | solution.py:187
  32.6 51.0 %collective-permute-start.3 = (bf16[2,3,64,256]{3,2,1,0:T(8,128)(2,1)S(1)}, bf16[2,3,64,256]{3,2,1,0:T(8,128)(2,1)S(1)}, u32[]{:S(2)}, u32[]{:S(2)}) collective-permute-start(bf16[2,3,64,256]{3,2,1,0:T(8,128)(2,1)S(1)} %get-tuple-element.142), channel_id=1, source_target_pairs={{0,4},{1,5},{2,6},{3,7},{4,0},{5,1},{6,2},{7,3},{8,12},{9,13},{10,... | collective-permute-start | bytes 589832 | tf_op jit(solution)/shard_map/in_near_4/ppermute | solution.py:187
  39.6 26.7 %collective-permute-start.6 = (bf16[2,3,128,256]{3,2,1,0:T(8,128)(2,1)S(1)}, bf16[2,3,128,256]{3,2,1,0:T(8,128)(2,1)S(1)}, u32[]{:S(2)}, u32[]{:S(2)}) collective-permute-start(bf16[2,3,128,256]{3,2,1,0:T(8,128)(2,1)S(1)} %get-tuple-element.140), channel_id=1, source_target_pairs={{0,4},{1,5},{2,6},{3,7},{4,0},{5,1},{6,2},{7,3},{8,12},{9,13},{10,... | collective-permute-start | bytes 1179656 | tf_op jit(solution)/shard_map/in_near_2/ppermute | solution.py:187
  39.8 26.6 %collective-permute-start.7 = (bf16[2,3,128,256]{3,2,1,0:T(8,128)(2,1)S(1)}, bf16[2,3,128,256]{3,2,1,0:T(8,128)(2,1)S(1)}, u32[]{:S(2)}, u32[]{:S(2)}) collective-permute-start(bf16[2,3,128,256]{3,2,1,0:T(8,128)(2,1)S(1)} %get-tuple-element.139), channel_id=1, source_target_pairs={{0,252},{1,253},{2,254},{3,255},{4,8},{5,9},{6,10},{7,11},{8,4},{9... | collective-permute-start | bytes 1179656 | tf_op jit(solution)/shard_map/in_far_2/ppermute | solution.py:187
  43.2 6.4 %copy-start.2 = (bf16[4,320,256]{2,1,0:T(8,128)(2,1)S(1)}, bf16[4,320,256]{2,1,0:T(8,128)(2,1)}, u32[]{:S(2)}) copy-start(bf16[4,320,256]{2,1,0:T(8,128)(2,1)} %q_ref.5) | copy-start | bytes 1966084
  43.2 6.4 %copy-start.3 = (s32[4,7]{1,0:T(4,128)S(1)}, s32[4,7]{1,0:T(4,128)}, u32[]{:S(2)}) copy-start(s32[4,7]{1,0:T(4,128)} %vis_ref.5) | copy-start | bytes 340
  43.2 45.3 %collective-permute-start.10 = (bf16[2,3,64,256]{3,2,1,0:T(8,128)(2,1)S(1)}, bf16[2,3,64,256]{3,2,1,0:T(8,128)(2,1)S(1)}, u32[]{:S(2)}, u32[]{:S(2)}) collective-permute-start(bf16[2,3,64,256]{3,2,1,0:T(8,128)(2,1)S(1)} %get-tuple-element.141), channel_id=1, source_target_pairs={{0,252},{1,253},{2,254},{3,255},{4,8},{5,9},{6,10},{7,11},{8,4},{9... | collective-permute-start | bytes 589832 | tf_op jit(solution)/shard_map/in_far_4/ppermute | solution.py:187
  66.4 22.0 %collective-permute-start.8 = (bf16[2,3,128,256]{3,2,1,0:T(8,128)(2,1)S(1)}, bf16[2,3,128,256]{3,2,1,0:T(8,128)(2,1)S(1)}, u32[]{:S(2)}, u32[]{:S(2)}) collective-permute-start(bf16[2,3,128,256]{3,2,1,0:T(8,128)(2,1)S(1)} %get-tuple-element.104), channel_id=1, source_target_pairs={{0,4},{1,5},{2,6},{3,7},{4,0},{5,1},{6,2},{7,3},{8,12},{9,13},{10,... | collective-permute-start | bytes 1179656 | tf_op jit(solution)/shard_map/out_near_0/ppermute | solution.py:187
  66.7 21.7 %collective-permute-start.9 = (bf16[2,3,128,256]{3,2,1,0:T(8,128)(2,1)S(1)}, bf16[2,3,128,256]{3,2,1,0:T(8,128)(2,1)S(1)}, u32[]{:S(2)}, u32[]{:S(2)}) collective-permute-start(bf16[2,3,128,256]{3,2,1,0:T(8,128)(2,1)S(1)} %get-tuple-element.105), channel_id=1, source_target_pairs={{0,252},{1,253},{2,254},{3,255},{4,8},{5,9},{6,10},{7,11},{8,4},{9... | collective-permute-start | bytes 1179656 | tf_op jit(solution)/shard_map/out_far_0/ppermute | solution.py:187
  83.5 24.3 %collective-permute-start.11 = (bf16[2,3,128,256]{3,2,1,0:T(8,128)(2,1)S(1)}, bf16[2,3,128,256]{3,2,1,0:T(8,128)(2,1)S(1)}, u32[]{:S(2)}, u32[]{:S(2)}) collective-permute-start(bf16[2,3,128,256]{3,2,1,0:T(8,128)(2,1)S(1)} %get-tuple-element.117), channel_id=1, source_target_pairs={{0,4},{1,5},{2,6},{3,7},{4,0},{5,1},{6,2},{7,3},{8,12},{9,13},{10,... | collective-permute-start | bytes 1179656 | tf_op jit(solution)/shard_map/out_near_2/ppermute | solution.py:187
  83.6 24.2 %collective-permute-start.12 = (bf16[2,3,128,256]{3,2,1,0:T(8,128)(2,1)S(1)}, bf16[2,3,128,256]{3,2,1,0:T(8,128)(2,1)S(1)}, u32[]{:S(2)}, u32[]{:S(2)}) collective-permute-start(bf16[2,3,128,256]{3,2,1,0:T(8,128)(2,1)S(1)} %get-tuple-element.118), channel_id=1, source_target_pairs={{0,252},{1,253},{2,254},{3,255},{4,8},{5,9},{6,10},{7,11},{8,4},{9... | collective-permute-start | bytes 1179656 | tf_op jit(solution)/shard_map/out_far_2/ppermute | solution.py:187
  96.1 15.9 %collective-permute-start.13 = (bf16[2,3,64,256]{3,2,1,0:T(8,128)(2,1)S(1)}, bf16[2,3,64,256]{3,2,1,0:T(8,128)(2,1)S(1)}, u32[]{:S(2)}, u32[]{:S(2)}) collective-permute-start(bf16[2,3,64,256]{3,2,1,0:T(8,128)(2,1)S(1)} %get-tuple-element.119), channel_id=1, source_target_pairs={{0,4},{1,5},{2,6},{3,7},{4,0},{5,1},{6,2},{7,3},{8,12},{9,13},{10,... | collective-permute-start | bytes 589832 | tf_op jit(solution)/shard_map/out_near_4/ppermute | solution.py:187
  96.2 15.8 %collective-permute-start.14 = (bf16[2,3,64,256]{3,2,1,0:T(8,128)(2,1)S(1)}, bf16[2,3,64,256]{3,2,1,0:T(8,128)(2,1)S(1)}, u32[]{:S(2)}, u32[]{:S(2)}) collective-permute-start(bf16[2,3,64,256]{3,2,1,0:T(8,128)(2,1)S(1)} %get-tuple-element.120), channel_id=1, source_target_pairs={{0,252},{1,253},{2,254},{3,255},{4,8},{5,9},{6,10},{7,11},{8,4},{9... | collective-permute-start | bytes 589832 | tf_op jit(solution)/shard_map/out_far_4/ppermute | solution.py:187

commit v4 on v3

--- a/solution.py
+++ b/solution.py
@@ -7,7 +7,7 @@
 
 DH = 64
 R = 3
-STRIP = 64
+STRIP = 16
 GROUPS = ((2, True), (2, False), (1, False))
 PARTS = ((2, False), (2, False), (1, False))
 
@@ -123,7 +123,7 @@
 
     for w in range(count):
         both = taken(R + w)
-        own_ref[0, w], own_ref[1, w] = both[:DH], both[DH:]
+        own_ref[0, w], own_ref[1, w] = both[:DH].astype(half), both[DH:].astype(half)
     for w in range(R):
         low, high = taken(w), taken(R + count + w)
         for ref, both in (
@@ -155,7 +155,7 @@
         out_specs=[own, block(2, count, at=first), block(2, R), block(2, R)],
         out_shape=[
             jax.ShapeDtypeStruct(queries.shape, half),
-            jax.ShapeDtypeStruct((2, *queries.shape), single),
+            jax.ShapeDtypeStruct((2, *queries.shape), half),
             jax.ShapeDtypeStruct((2, R, width, T), half),
             jax.ShapeDtypeStruct((2, R, width, T), half),
         ],
@@ -276,7 +276,7 @@
     backs[-2:] = [tail[: len(backs[-2])], tail[len(backs[-2]) :]]
     sums = []
     for (first, heads, _), (near, *far) in zip(spans(PARTS), backs):
-        mine = own[:, :, first * DH : (first + heads) * DH]
+        mine = own[:, :, first * DH : (first + heads) * DH].astype(single)
         if not far:
             mine = mine + near.astype(single)
         else:

time: 115 us -> 114 us (level)
  transfers between devices with their start and end apart: 15 -> 15, of which waited for: 5 -> 5; matrix products, arithmetic and copies ran while one was open for 8% -> 9% of each run, Pallas kernels for 32% -> 31%
where the time goes in v4:
time: 114 us
  starting transfers between devices  37.9 us (33%)
  Pallas kernels  35.9 us (31%)
  waiting for transfers between devices  27.4 us (24%)
  local copies, waits for them, and re-layouts  5.9 us (5%)
  other arithmetic  3.58 us (3%)
  matrix products  2.5 us (2%)
    ppermute x15, starting transfers between devices, send(): return lax.ppermute(array, ('view', 'head'), pairs)  37.9 us
    pallas_call x3, Pallas kernels, attn(): pl.pallas_call(attn_kernel, grid=(heads,), in_specs=[smem, smem, own, own...  35.9 us
    ppermute x15, waiting for transfers between devices, send(): return lax.ppermute(array, ('view', 'head'), pairs)  27.4 us
    dot_general x1, matrix products, local(): jnp.einsum('ij,vjt->vit', weight, gathered, preferred_element_type=single)  2.5 us
  transfers between devices with their start and end apart: 15, of which 5 were waited for; matrix products, arithmetic and copies ran while one was open for 9% of the time, Pallas kernels for 31%

profile of v4, /device:TPU:1, one launch (start us, length us, event | category | flops | bytes accessed | tf_op | source)
XLA Modules:
  0.0 114.0 jit_solution(871522595856975164)
XLA Ops:
  0.6 0.0 copy-start
  0.6 0.0 copy-start.1
  0.7 2.1 %collective-permute-start.1 = (bf16[4,320,256]{2,1,0:T(8,128)(2,1)}, bf16[4,320,256]{2,1,0:T(8,128)(2,1)}, u32[]{:S(2)}, u32[]{:S(2)}) collective-permute-start(bf16[4,320,256]{2,1,0:T(8,128)(2,1)} %param.21), channel_id=1, source_target_pairs={{0,2},{1,3},{2,0},{3,1},{4,6},{5,7},{6,4},{7,5},{8,10},{9,11},{10,... | collective-permute-start | bytes 1966088 | tf_op jit(solution)/shard_map/beside/ppermute | solution.py:187
  2.8 1.3 %collective-permute-start = (bf16[4,320,256]{2,1,0:T(8,128)(2,1)}, bf16[4,320,256]{2,1,0:T(8,128)(2,1)}, u32[]{:S(2)}, u32[]{:S(2)}) collective-permute-start(bf16[4,320,256]{2,1,0:T(8,128)(2,1)} %param.21), channel_id=1, source_target_pairs={{0,1},{1,0},{2,3},{3,2},{4,5},{5,4},{6,7},{7,6},{8,9},{9,8},{10,11... | collective-permute-start | bytes 1966088 | tf_op jit(solution)/shard_map/twin/ppermute | solution.py:187
  4.1 1.3 %slice_bitcast_fusion.2 = (bf16[1,4,128,256]{3,2,1,0:T(8,128)(2,1)S(1)}, bf16[1,4,128,256]{3,2,1,0:T(8,128)(2,1)S(1)}, bf16[1,4,128,256]{3,2,1,0:T(8,128)(2,1)S(1)}, bf16[1,4,128,256]{3,2,1,0:T(8,128)(2,1)S(1)}) fusion(bf16[4,320,256]{2,1,0:T(8,128)(2,1)} %v_ref.5, bf16[4,320,256]{2,1,0:T(8,128)(2,1)} %k_ref.5), kind=kLoop, calls=%fused_computation.32 | loop fusion | bytes 2097152 | tf_op jit(solution)/shard_map/stack | solution.py:224
  5.3 0.0 copy-start.4
  5.4 0.8 pad_maximum_fusion.1
  6.2 2.1 %collective-permute-start.4 = (bf16[2,4,128,256]{3,2,1,0:T(8,128)(2,1)}, bf16[2,4,128,256]{3,2,1,0:T(8,128)(2,1)S(1)}, u32[]{:S(2)}, u32[]{:S(2)}) collective-permute-start(bf16[2,4,128,256]{3,2,1,0:T(8,128)(2,1)} %pad_maximum_fusion.1), channel_id=1, source_target_pairs={{0,4},{1,5},{2,6},{3,7},{4,0},{5,1},{6,2},{7,3},{8,12},{9,13},{10,... | collective-permute-start | bytes 1572872 | tf_op jit(solution)/shard_map/in_near_0/ppermute | solution.py:187
  8.3 0.0 copy-done
  8.3 0.0 copy-done.1
  8.3 0.7 slice_bitcast_fusion.6
  9.0 7.2 %collective-permute-done.1 = bf16[4,320,256]{2,1,0:T(8,128)(2,1)} collective-permute-done((bf16[4,320,256]{2,1,0:T(8,128)(2,1)}, bf16[4,320,256]{2,1,0:T(8,128)(2,1)}, u32[]{:S(2)}, u32[]{:S(2)}) %collective-permute-start.1) | collective-permute-done | bytes 655392 | tf_op jit(solution)/shard_map/beside/ppermute | solution.py:187
  16.2 5.8 %collective-permute-start.2 = (bf16[4,320,256]{2,1,0:T(8,128)(2,1)}, bf16[4,320,256]{2,1,0:T(8,128)(2,1)}, u32[]{:S(2)}, u32[]{:S(2)}) collective-permute-start(bf16[4,320,256]{2,1,0:T(8,128)(2,1)} %collective-permute-done.1), channel_id=1, source_target_pairs={{0,1},{1,0},{2,3},{3,2},{4,5},{5,4},{6,7},{7,6},{8,9},{9,8},{10,11... | collective-permute-start | bytes 1966088 | tf_op jit(solution)/shard_map/across/ppermute | solution.py:187
  22.0 0.0 copy-done.4
  22.0 1.3 %constant_dynamic-slice_fusion.5 = (bf16[320,320]{1,0:T(8,128)(2,1)S(1)}, bf16[320,320]{1,0:T(8,128)(2,1)}, bf16[320,320]{1,0:T(8,128)(2,1)}, bf16[320,320]{1,0:T(8,128)(2,1)}) fusion(bf16[320,1280]{1,0:T(8,128)(2,1)S(1)} %copy-done.4, s32[]{:T(128)S(6)} %select_n.64, s32[]{:T(128)S(6)} %select_n.62, s32[]{:T(128)S(6)} %select_n.61, s32[]{:T(128)S(6)} %select_n.63), kind=kLoop, calls=%fused_computation.43 | loop fusion | bytes 1638416 | tf_op jit(solution)/shard_map/dynamic_slice | solution.py:244
  23.2 1.4 %concatenate.22 = bf16[320,1280]{1,0:T(8,128)(2,1)S(1)} concatenate(bf16[320,320]{1,0:T(8,128)(2,1)} %get-tuple-element.131, bf16[320,320]{1,0:T(8,128)(2,1)} %get-tuple-element.130, bf16[320,320]{1,0:T(8,128)(2,1)} %get-tuple-element.132, bf16[320,320]{1,0:T(8,128)(2,1)S(1)} %get-tuple-element.129), dimensions={1} | concatenate | bytes 1638400 | tf_op jit(solution)/shard_map/concatenate | solution.py:243
  24.7 0.9 pad_maximum_fusion.3
  25.6 0.1 pad_maximum_fusion.2
  25.7 5.1 %collective-permute-done.4.near_ref = bf16[2,4,128,256]{3,2,1,0:T(8,128)(2,1)S(1)} collective-permute-done((bf16[2,4,128,256]{3,2,1,0:T(8,128)(2,1)}, bf16[2,4,128,256]{3,2,1,0:T(8,128)(2,1)S(1)}, u32[]{:S(2)}, u32[]{:S(2)}) %collective-permute-start.4) | collective-permute-done | bytes 524320 | tf_op jit(solution)/shard_map/in_near_0/ppermute | solution.py:187
  30.8 0.0 copy-start.5
  30.9 1.7 %collective-permute-start.5 = (bf16[2,3,128,256]{3,2,1,0:T(8,128)(2,1)S(1)}, bf16[2,3,128,256]{3,2,1,0:T(8,128)(2,1)S(1)}, u32[]{:S(2)}, u32[]{:S(2)}) collective-permute-start(bf16[2,3,128,256]{3,2,1,0:T(8,128)(2,1)S(1)} %constant_dynamic-slice_fusion.3), channel_id=1, source_target_pairs={{0,8},{1,9},{2,10},{3,11},{4,252},{5,253},{6,254},{7,255},{8,16},{... | collective-permute-start | bytes 1179656 | tf_op jit(solution)/shard_map/in_far_0/ppermute | solution.py:187
  32.6 7.0 %collective-permute-start.3 = (bf16[2,3,64,256]{3,2,1,0:T(8,128)(2,1)S(1)}, bf16[2,3,64,256]{3,2,1,0:T(8,128)(2,1)S(1)}, u32[]{:S(2)}, u32[]{:S(2)}) collective-permute-start(bf16[2,3,64,256]{3,2,1,0:T(8,128)(2,1)S(1)} %get-tuple-element.140), channel_id=1, source_target_pairs={{0,4},{1,5},{2,6},{3,7},{4,0},{5,1},{6,2},{7,3},{8,12},{9,13},{10,... | collective-permute-start | bytes 589832 | tf_op jit(solution)/shard_map/in_near_4/ppermute | solution.py:187
  39.6 0.1 constant_dynamic-slice_fusion.1
  39.7 0.1 collective-permute-start.6
  39.8 0.0 collective-permute-done
  39.8 3.4 %collective-permute-start.7 = (bf16[2,3,128,256]{3,2,1,0:T(8,128)(2,1)S(1)}, bf16[2,3,128,256]{3,2,1,0:T(8,128)(2,1)S(1)}, u32[]{:S(2)}, u32[]{:S(2)}) collective-permute-start(bf16[2,3,128,256]{3,2,1,0:T(8,128)(2,1)S(1)} %get-tuple-element.137), channel_id=1, source_target_pairs={{0,252},{1,253},{2,254},{3,255},{4,8},{5,9},{6,10},{7,11},{8,4},{9... | collective-permute-start | bytes 1179656 | tf_op jit(solution)/shard_map/in_far_2/ppermute | solution.py:187
  43.2 0.0 collective-permute-done.2
  43.2 0.0 copy-start.2
  43.2 3.9 %collective-permute-start.10 = (bf16[2,3,64,256]{3,2,1,0:T(8,128)(2,1)S(1)}, bf16[2,3,64,256]{3,2,1,0:T(8,128)(2,1)S(1)}, u32[]{:S(2)}, u32[]{:S(2)}) collective-permute-start(bf16[2,3,64,256]{3,2,1,0:T(8,128)(2,1)S(1)} %get-tuple-element.139), channel_id=1, source_target_pairs={{0,252},{1,253},{2,254},{3,255},{4,8},{5,9},{6,10},{7,11},{8,4},{9... | collective-permute-start | bytes 589832 | tf_op jit(solution)/shard_map/in_far_4/ppermute | solution.py:187
  47.0 0.0 copy-done.5
  47.1 2.5 %fusion.11.g_ref = bf16[4,320,256]{2,1,0:T(8,128)(2,1)S(1)} fusion(bf16[4,320,256]{2,1,0:T(8,128)(2,1)} %collective-permute-done.2, bf16[4,320,256]{2,1,0:T(8,128)(2,1)} %collective-permute-done.1, bf16[4,320,256]{2,1,0:T(8,128)(2,1)} %collective-permute-done, bf16[4,320,256]{2,1,0:T(8,128)(2,1)S(1)} %copy-done.5, bf16[320,1280]{1,0:T(8,128)(2,1)S(1)} %concatenate.22), kind=kOutput, calls=%fused_computation.10 | convolution fusion | flops 849674240 | bytes 4096000 | tf_op jit(solution)/shard_map/ij,vjt->vit/dot_general | solution.py:247
  49.6 0.0 collective-permute-done.5.far_ref
  49.6 0.0 copy-done.2
  49.6 0.0 copy-done.3
  49.6 14.2 %shard_map.85 = (bf16[4,320,256]{2,1,0:T(8,128)(2,1)}, bf16[2,4,320,256]{3,2,1,0:T(8,128)(2,1)S(1)}, bf16[2,3,128,256]{3,2,1,0:T(8,128)(2,1)S(1)}, bf16[2,3,128,256]{3,2,1,0:T(8,128)(2,1)S(1)}) custom-call(s32[4,7]{1,0:T(4,128)S(1)} %copy-done.3, s32[1]{0:T(128)} %bitcast.col_ref, bf16[4,320,256]{2,1,0:T(8,128)(2,1)S(1)} %copy-done.2, ...), custom_call_target="tpu_custom_call" | custom-call | flops 9395240960 | bytes 8388608 | tf_op jit(solution)/shard_map/pallas_call | solution.py:150
  63.7 2.6 %collective-permute-done.6.near_ref = bf16[2,3,128,256]{3,2,1,0:T(8,128)(2,1)S(1)} collective-permute-done((bf16[2,3,128,256]{3,2,1,0:T(8,128)(2,1)S(1)}, bf16[2,3,128,256]{3,2,1,0:T(8,128)(2,1)S(1)}, u32[]{:S(2)}, u32[]{:S(2)}) %collective-permute-start.6) | collective-permute-done | bytes 393248 | tf_op jit(solution)/shard_map/in_near_2/ppermute | solution.py:187
  66.4 0.0 collective-permute-done.7.far_ref
  66.4 0.4 collective-permute-start.8
  66.7 2.5 %collective-permute-start.9 = (bf16[2,3,128,256]{3,2,1,0:T(8,128)(2,1)S(1)}, bf16[2,3,128,256]{3,2,1,0:T(8,128)(2,1)S(1)}, u32[]{:S(2)}, u32[]{:S(2)}) collective-permute-start(bf16[2,3,128,256]{3,2,1,0:T(8,128)(2,1)S(1)} %get-tuple-element.105), channel_id=1, source_target_pairs={{0,252},{1,253},{2,254},{3,255},{4,8},{5,9},{6,10},{7,11},{8,4},{9... | collective-permute-start | bytes 1179656 | tf_op jit(solution)/shard_map/out_far_0/ppermute | solution.py:187
  69.2 14.1 %shard_map.86 = (bf16[4,320,256]{2,1,0:T(8,128)(2,1)}, bf16[2,4,320,256]{3,2,1,0:T(8,128)(2,1)S(1)}, bf16[2,3,128,256]{3,2,1,0:T(8,128)(2,1)S(1)}, bf16[2,3,128,256]{3,2,1,0:T(8,128)(2,1)S(1)}) custom-call(s32[4,7]{1,0:T(4,128)S(1)} %copy-done.3, s32[1]{0:T(128)} %bitcast.col_ref, ...), custom_call_target="tpu_custom_call", output_to_operand_aliasing={{0}: (8, {}), {1}: (9, {})} | custom-call | flops 9395240960 | bytes 8388608 | tf_op jit(solution)/shard_map/pallas_call | solution.py:150
  83.3 0.1 collective-permute-start.11
  83.5 0.0 collective-permute-done.3.near_ref
  83.5 4.8 %collective-permute-start.12 = (bf16[2,3,128,256]{3,2,1,0:T(8,128)(2,1)S(1)}, bf16[2,3,128,256]{3,2,1,0:T(8,128)(2,1)S(1)}, u32[]{:S(2)}, u32[]{:S(2)}) collective-permute-start(bf16[2,3,128,256]{3,2,1,0:T(8,128)(2,1)S(1)} %get-tuple-element.118), channel_id=1, source_target_pairs={{0,252},{1,253},{2,254},{3,255},{4,8},{5,9},{6,10},{7,11},{8,4},{9... | collective-permute-start | bytes 1179656 | tf_op jit(solution)/shard_map/out_far_2/ppermute | solution.py:187
  88.3 0.0 collective-permute-done.8
  88.3 0.0 collective-permute-done.9
  88.3 0.0 collective-permute-done.10.far_ref
  88.3 7.6 %shard_map.87 = (bf16[4,320,256]{2,1,0:T(8,128)(2,1)}, bf16[2,4,320,256]{3,2,1,0:T(8,128)(2,1)S(1)}, bf16[2,3,64,256]{3,2,1,0:T(8,128)(2,1)S(1)}, bf16[2,3,64,256]{3,2,1,0:T(8,128)(2,1)S(1)}) custom-call(s32[4,7]{1,0:T(4,128)S(1)} %copy-done.3, s32[1]{0:T(128)} %bitcast.col_ref, ...), custom_call_target="tpu_custom_call", output_to_operand_aliasing={{0}: (8, {}), {1}: (9, {})} | custom-call | flops 4697620480 | bytes 4194304 | tf_op jit(solution)/shard_map/pallas_call | solution.py:150
  95.9 0.0 collective-permute-start.13
  95.9 2.8 %collective-permute-start.14 = (bf16[2,3,64,256]{3,2,1,0:T(8,128)(2,1)S(1)}, bf16[2,3,64,256]{3,2,1,0:T(8,128)(2,1)S(1)}, u32[]{:S(2)}, u32[]{:S(2)}) collective-permute-start(bf16[2,3,64,256]{3,2,1,0:T(8,128)(2,1)S(1)} %get-tuple-element.120), channel_id=1, source_target_pairs={{0,252},{1,253},{2,254},{3,255},{4,8},{5,9},{6,10},{7,11},{8,4},{9... | collective-permute-start | bytes 589832 | tf_op jit(solution)/shard_map/out_far_4/ppermute | solution.py:187
  98.7 0.2 slice_convert_fusion.1
  98.9 0.3 fusion.18
  99.1 0.3 fusion.17
  99.4 0.1 convert_element_type.46
  99.5 8.2 %collective-permute-done.11 = bf16[2,3,128,256]{3,2,1,0:T(8,128)(2,1)S(1)} collective-permute-done((bf16[2,3,128,256]{3,2,1,0:T(8,128)(2,1)S(1)}, bf16[2,3,128,256]{3,2,1,0:T(8,128)(2,1)S(1)}, u32[]{:S(2)}, u32[]{:S(2)}) %collective-permute-start.11) | collective-permute-done | bytes 393248 | tf_op jit(solution)/shard_map/out_near_2/ppermute | solution.py:187
  107.7 0.0 collective-permute-done.12
  107.7 4.2 %collective-permute-done.13 = bf16[2,3,64,256]{3,2,1,0:T(8,128)(2,1)S(1)} collective-permute-done((bf16[2,3,64,256]{3,2,1,0:T(8,128)(2,1)S(1)}, bf16[2,3,64,256]{3,2,1,0:T(8,128)(2,1)S(1)}, u32[]{:S(2)}, u32[]{:S(2)}) %collective-permute-start.13) | collective-permute-done | bytes 196640 | tf_op jit(solution)/shard_map/out_near_4/ppermute | solution.py:187
  111.9 0.0 collective-permute-done.14
  111.9 0.1 fusion.20
  112.0 0.1 fusion.19
  112.2 0.3 fusion.16
  112.5 0.3 fusion.15
  112.7 0.1 convert_element_type.50
  112.8 0.1 pad_maximum_fusion
  112.9 1.1 %slice_bitcast_fusion = (bf16[4,320,256]{2,1,0:T(8,128)(2,1)}, bf16[4,320,256]{2,1,0:T(8,128)(2,1)}) fusion(bf16[2,4,320,256]{3,2,1,0:T(8,128)(2,1)S(1)} %pad_maximum_fusion), kind=kLoop, calls=%fused_computation.20 | loop fusion | bytes 2621440 | tf_op jit(solution)/shard_map/squeeze | solution.py:288
  (5 shorter events, 0.1 us)
Async XLA Ops:
  0.6 7.7 %copy-start = (bf16[4,320,256]{2,1,0:T(8,128)(2,1)S(1)}, bf16[4,320,256]{2,1,0:T(8,128)(2,1)}, u32[]{:S(2)}) copy-start(bf16[4,320,256]{2,1,0:T(8,128)(2,1)} %k_ref.5) | copy-start | bytes 1966084
  0.6 7.7 %copy-start.1 = (bf16[4,320,256]{2,1,0:T(8,128)(2,1)S(1)}, bf16[4,320,256]{2,1,0:T(8,128)(2,1)}, u32[]{:S(2)}) copy-start(bf16[4,320,256]{2,1,0:T(8,128)(2,1)} %v_ref.5) | copy-start | bytes 1966084
  0.7 15.5 %collective-permute-start.1 = (bf16[4,320,256]{2,1,0:T(8,128)(2,1)}, bf16[4,320,256]{2,1,0:T(8,128)(2,1)}, u32[]{:S(2)}, u32[]{:S(2)}) collective-permute-start(bf16[4,320,256]{2,1,0:T(8,128)(2,1)} %param.21), channel_id=1, source_target_pairs={{0,2},{1,3},{2,0},{3,1},{4,6},{5,7},{6,4},{7,5},{8,10},{9,11},{10,... | collective-permute-start | bytes 1966088 | tf_op jit(solution)/shard_map/beside/ppermute | solution.py:187
  2.8 37.0 %collective-permute-start = (bf16[4,320,256]{2,1,0:T(8,128)(2,1)}, bf16[4,320,256]{2,1,0:T(8,128)(2,1)}, u32[]{:S(2)}, u32[]{:S(2)}) collective-permute-start(bf16[4,320,256]{2,1,0:T(8,128)(2,1)} %param.21), channel_id=1, source_target_pairs={{0,1},{1,0},{2,3},{3,2},{4,5},{5,4},{6,7},{7,6},{8,9},{9,8},{10,11... | collective-permute-start | bytes 1966088 | tf_op jit(solution)/shard_map/twin/ppermute | solution.py:187
  5.3 16.6 %copy-start.4 = (bf16[320,1280]{1,0:T(8,128)(2,1)S(1)}, bf16[320,1280]{1,0:T(8,128)(2,1)}, u32[]{:S(2)}) copy-start(bf16[320,1280]{1,0:T(8,128)(2,1)} %param.22) | copy-start | bytes 2457604
  6.2 24.6 %collective-permute-start.4 = (bf16[2,4,128,256]{3,2,1,0:T(8,128)(2,1)}, bf16[2,4,128,256]{3,2,1,0:T(8,128)(2,1)S(1)}, u32[]{:S(2)}, u32[]{:S(2)}) collective-permute-start(bf16[2,4,128,256]{3,2,1,0:T(8,128)(2,1)} %pad_maximum_fusion.1), channel_id=1, source_target_pairs={{0,4},{1,5},{2,6},{3,7},{4,0},{5,1},{6,2},{7,3},{8,12},{9,13},{10,... | collective-permute-start | bytes 1572872 | tf_op jit(solution)/shard_map/in_near_0/ppermute | solution.py:187
  16.2 27.0 %collective-permute-start.2 = (bf16[4,320,256]{2,1,0:T(8,128)(2,1)}, bf16[4,320,256]{2,1,0:T(8,128)(2,1)}, u32[]{:S(2)}, u32[]{:S(2)}) collective-permute-start(bf16[4,320,256]{2,1,0:T(8,128)(2,1)} %collective-permute-done.1), channel_id=1, source_target_pairs={{0,1},{1,0},{2,3},{3,2},{4,5},{5,4},{6,7},{7,6},{8,9},{9,8},{10,11... | collective-permute-start | bytes 1966088 | tf_op jit(solution)/shard_map/across/ppermute | solution.py:187
  30.8 16.2 %copy-start.5 = (bf16[4,320,256]{2,1,0:T(8,128)(2,1)S(1)}, bf16[4,320,256]{2,1,0:T(8,128)(2,1)}, u32[]{:S(2)}) copy-start(bf16[4,320,256]{2,1,0:T(8,128)(2,1)} %param.21) | copy-start | bytes 1966084
  30.9 18.7 %collective-permute-start.5 = (bf16[2,3,128,256]{3,2,1,0:T(8,128)(2,1)S(1)}, bf16[2,3,128,256]{3,2,1,0:T(8,128)(2,1)S(1)}, u32[]{:S(2)}, u32[]{:S(2)}) collective-permute-start(bf16[2,3,128,256]{3,2,1,0:T(8,128)(2,1)S(1)} %constant_dynamic-slice_fusion.3), channel_id=1, source_target_pairs={{0,8},{1,9},{2,10},{3,11},{4,252},{5,253},{6,254},{7,255},{8,16},{... | collective-permute-start | bytes 1179656 | tf_op jit(solution)/shard_map/in_far_0/ppermute | solution.py:187
  32.6 50.9 %collective-permute-start.3 = (bf16[2,3,64,256]{3,2,1,0:T(8,128)(2,1)S(1)}, bf16[2,3,64,256]{3,2,1,0:T(8,128)(2,1)S(1)}, u32[]{:S(2)}, u32[]{:S(2)}) collective-permute-start(bf16[2,3,64,256]{3,2,1,0:T(8,128)(2,1)S(1)} %get-tuple-element.140), channel_id=1, source_target_pairs={{0,4},{1,5},{2,6},{3,7},{4,0},{5,1},{6,2},{7,3},{8,12},{9,13},{10,... | collective-permute-start | bytes 589832 | tf_op jit(solution)/shard_map/in_near_4/ppermute | solution.py:187
  39.7 26.7 %collective-permute-start.6 = (bf16[2,3,128,256]{3,2,1,0:T(8,128)(2,1)S(1)}, bf16[2,3,128,256]{3,2,1,0:T(8,128)(2,1)S(1)}, u32[]{:S(2)}, u32[]{:S(2)}) collective-permute-start(bf16[2,3,128,256]{3,2,1,0:T(8,128)(2,1)S(1)} %get-tuple-element.138), channel_id=1, source_target_pairs={{0,4},{1,5},{2,6},{3,7},{4,0},{5,1},{6,2},{7,3},{8,12},{9,13},{10,... | collective-permute-start | bytes 1179656 | tf_op jit(solution)/shard_map/in_near_2/ppermute | solution.py:187
  39.8 26.6 %collective-permute-start.7 = (bf16[2,3,128,256]{3,2,1,0:T(8,128)(2,1)S(1)}, bf16[2,3,128,256]{3,2,1,0:T(8,128)(2,1)S(1)}, u32[]{:S(2)}, u32[]{:S(2)}) collective-permute-start(bf16[2,3,128,256]{3,2,1,0:T(8,128)(2,1)S(1)} %get-tuple-element.137), channel_id=1, source_target_pairs={{0,252},{1,253},{2,254},{3,255},{4,8},{5,9},{6,10},{7,11},{8,4},{9... | collective-permute-start | bytes 1179656 | tf_op jit(solution)/shard_map/in_far_2/ppermute | solution.py:187
  43.2 6.4 %copy-start.2 = (bf16[4,320,256]{2,1,0:T(8,128)(2,1)S(1)}, bf16[4,320,256]{2,1,0:T(8,128)(2,1)}, u32[]{:S(2)}) copy-start(bf16[4,320,256]{2,1,0:T(8,128)(2,1)} %q_ref.5) | copy-start | bytes 1966084
  43.2 6.4 %copy-start.3 = (s32[4,7]{1,0:T(4,128)S(1)}, s32[4,7]{1,0:T(4,128)}, u32[]{:S(2)}) copy-start(s32[4,7]{1,0:T(4,128)} %vis_ref.5) | copy-start | bytes 340
  43.2 45.1 %collective-permute-start.10 = (bf16[2,3,64,256]{3,2,1,0:T(8,128)(2,1)S(1)}, bf16[2,3,64,256]{3,2,1,0:T(8,128)(2,1)S(1)}, u32[]{:S(2)}, u32[]{:S(2)}) collective-permute-start(bf16[2,3,64,256]{3,2,1,0:T(8,128)(2,1)S(1)} %get-tuple-element.139), channel_id=1, source_target_pairs={{0,252},{1,253},{2,254},{3,255},{4,8},{5,9},{6,10},{7,11},{8,4},{9... | collective-permute-start | bytes 589832 | tf_op jit(solution)/shard_map/in_far_4/ppermute | solution.py:187
  66.4 21.9 %collective-permute-start.8 = (bf16[2,3,128,256]{3,2,1,0:T(8,128)(2,1)S(1)}, bf16[2,3,128,256]{3,2,1,0:T(8,128)(2,1)S(1)}, u32[]{:S(2)}, u32[]{:S(2)}) collective-permute-start(bf16[2,3,128,256]{3,2,1,0:T(8,128)(2,1)S(1)} %get-tuple-element.104), channel_id=1, source_target_pairs={{0,4},{1,5},{2,6},{3,7},{4,0},{5,1},{6,2},{7,3},{8,12},{9,13},{10,... | collective-permute-start | bytes 1179656 | tf_op jit(solution)/shard_map/out_near_0/ppermute | solution.py:187
  66.7 21.5 %collective-permute-start.9 = (bf16[2,3,128,256]{3,2,1,0:T(8,128)(2,1)S(1)}, bf16[2,3,128,256]{3,2,1,0:T(8,128)(2,1)S(1)}, u32[]{:S(2)}, u32[]{:S(2)}) collective-permute-start(bf16[2,3,128,256]{3,2,1,0:T(8,128)(2,1)S(1)} %get-tuple-element.105), channel_id=1, source_target_pairs={{0,252},{1,253},{2,254},{3,255},{4,8},{5,9},{6,10},{7,11},{8,4},{9... | collective-permute-start | bytes 1179656 | tf_op jit(solution)/shard_map/out_far_0/ppermute | solution.py:187
  83.3 24.3 %collective-permute-start.11 = (bf16[2,3,128,256]{3,2,1,0:T(8,128)(2,1)S(1)}, bf16[2,3,128,256]{3,2,1,0:T(8,128)(2,1)S(1)}, u32[]{:S(2)}, u32[]{:S(2)}) collective-permute-start(bf16[2,3,128,256]{3,2,1,0:T(8,128)(2,1)S(1)} %get-tuple-element.117), channel_id=1, source_target_pairs={{0,4},{1,5},{2,6},{3,7},{4,0},{5,1},{6,2},{7,3},{8,12},{9,13},{10,... | collective-permute-start | bytes 1179656 | tf_op jit(solution)/shard_map/out_near_2/ppermute | solution.py:187
  83.5 24.2 %collective-permute-start.12 = (bf16[2,3,128,256]{3,2,1,0:T(8,128)(2,1)S(1)}, bf16[2,3,128,256]{3,2,1,0:T(8,128)(2,1)S(1)}, u32[]{:S(2)}, u32[]{:S(2)}) collective-permute-start(bf16[2,3,128,256]{3,2,1,0:T(8,128)(2,1)S(1)} %get-tuple-element.118), channel_id=1, source_target_pairs={{0,252},{1,253},{2,254},{3,255},{4,8},{5,9},{6,10},{7,11},{8,4},{9... | collective-permute-start | bytes 1179656 | tf_op jit(solution)/shard_map/out_far_2/ppermute | solution.py:187
  95.9 16.0 %collective-permute-start.13 = (bf16[2,3,64,256]{3,2,1,0:T(8,128)(2,1)S(1)}, bf16[2,3,64,256]{3,2,1,0:T(8,128)(2,1)S(1)}, u32[]{:S(2)}, u32[]{:S(2)}) collective-permute-start(bf16[2,3,64,256]{3,2,1,0:T(8,128)(2,1)S(1)} %get-tuple-element.119), channel_id=1, source_target_pairs={{0,4},{1,5},{2,6},{3,7},{4,0},{5,1},{6,2},{7,3},{8,12},{9,13},{10,... | collective-permute-start | bytes 589832 | tf_op jit(solution)/shard_map/out_near_4/ppermute | solution.py:187
  95.9 16.0 %collective-permute-start.14 = (bf16[2,3,64,256]{3,2,1,0:T(8,128)(2,1)S(1)}, bf16[2,3,64,256]{3,2,1,0:T(8,128)(2,1)S(1)}, u32[]{:S(2)}, u32[]{:S(2)}) collective-permute-start(bf16[2,3,64,256]{3,2,1,0:T(8,128)(2,1)S(1)} %get-tuple-element.120), channel_id=1, source_target_pairs={{0,252},{1,253},{2,254},{3,255},{4,8},{5,9},{6,10},{7,11},{8,4},{9... | collective-permute-start | bytes 589832 | tf_op jit(solution)/shard_map/out_far_4/ppermute | solution.py:187
